TPU v7x, 128 devices: a whole 4x4x4 slice. The times are simulated.
128 devices in a mesh: pipe: 2 (over x_hi), dp: 16 (over y, z), tensor: 4 (over x_lo, core).
Axes of the slice: x: 4 (x_hi: 2, x_lo: 2; x = x_hi * 2 + x_lo), y: 4, z: 4, core: 2. Of those that a mesh axis runs over, the one named last changes fastest.
Arguments:
- inputs: bfloat16 [8192, 1024], P('dp'), may hold values from -6 to 6
- memories: bfloat16 [2, 16, 512, 1024], P('pipe', 'dp'), may hold values from -6 to 6
- compressed: bfloat16 [2, 16, 512, 1024], P('pipe', 'dp'), may hold values from -6 to 6
- documents: int32 [16, 1536], P('dp'), may hold values from 0 to 3, as said below
- cotangent: bfloat16 [8192, 1024], P('dp'), may hold values from -6 to 6
- compressed_cotangent: bfloat16 [2, 16, 256, 1024], P('pipe', 'dp', None, 'tensor'), may hold values from -6 to 6
- query_weight: bfloat16 [2, 1024, 1024], P('pipe', None, 'tensor'), may hold values from -0.1875 to 0.1875
- key_weight: bfloat16 [2, 1024, 1024], P('pipe', None, 'tensor'), may hold values from -0.1875 to 0.1875
- value_weight: bfloat16 [2, 1024, 1024], P('pipe', None, 'tensor'), may hold values from -0.1875 to 0.1875
- output_weight: bfloat16 [2, 1024, 1024], P('pipe', 'tensor'), may hold values from -3 to 3
- output_bias: bfloat16 [2, 1024], P('pipe'), may hold values from -2 to 2
- inner_weight: bfloat16 [2, 1024, 4096], P('pipe', None, 'tensor'), may hold values from -0.1875 to 0.1875
- inner_bias: bfloat16 [2, 4096], P('pipe', 'tensor'), may hold values from -2 to 2
- outer_weight: bfloat16 [2, 4096, 1024], P('pipe', 'tensor'), may hold values from -0.09375 to 0.09375
- outer_bias: bfloat16 [2, 1024], P('pipe'), may hold values from -2 to 2
- conv_weight: bfloat16 [2, 2, 1024, 1024], P('pipe', None, None, 'tensor'), may hold values from -0.125 to 0.125
- conv_bias: bfloat16 [2, 1024], P('pipe', 'tensor'), may hold values from -2 to 2
- attn_gain: bfloat16 [2, 1024], P('pipe'), may hold values from 0.5 to 1.5
- attn_shift: bfloat16 [2, 1024], P('pipe'), may hold values from -2 to 2
- ffn_gain: bfloat16 [2, 1024], P('pipe'), may hold values from 0.5 to 1.5
- ffn_shift: bfloat16 [2, 1024], P('pipe'), may hold values from -2 to 2
Outputs:
- hidden_states: float32 [2, 8192, 1024], P('pipe', 'dp')
- new_compressed: bfloat16 [2, 16, 512, 1024], P('pipe', 'dp', None, 'tensor')
- input_grads: float32 [2, 8192, 1024], P('pipe', 'dp')
- query_grad: float32 [2, 1024, 1024], P('pipe', None, 'tensor')
- key_grad: float32 [2, 1024, 1024], P('pipe', None, 'tensor')
- value_grad: float32 [2, 1024, 1024], P('pipe', None, 'tensor')
- output_grad: float32 [2, 1024, 1024], P('pipe', 'tensor')
- output_bias_grad: float32 [2, 1024], P('pipe')
- inner_grad: float32 [2, 1024, 4096], P('pipe', None, 'tensor')
- inner_bias_grad: float32 [2, 4096], P('pipe', 'tensor')
- outer_grad: float32 [2, 4096, 1024], P('pipe', 'tensor')
- outer_bias_grad: float32 [2, 1024], P('pipe')
- conv_grad: float32 [2, 2, 1024, 1024], P('pipe', None, None, 'tensor')
- conv_bias_grad: float32 [2, 1024], P('pipe', 'tensor')
- attn_gain_grad: float32 [2, 1024], P('pipe')
- attn_shift_grad: float32 [2, 1024], P('pipe')
- ffn_gain_grad: float32 [2, 1024], P('pipe')
- ffn_shift_grad: float32 [2, 1024], P('pipe')
Inputs may be any that keep to these rules, and one draw needn't show every extreme that they name: Each row of documents starts at 0, never falls from one position to the next, and holds exactly four documents.
All inputs are finite; a program needn't handle non-finite values.
Results may differ from a plain program's by a relative error of at most 0.015.
Values sent between devices are 32-bit elements; how exact they have to be, the bound alone decides.
No kernel may reach another device: no remote copies, remote signals or barrier semaphores. Data moves between devices by JAX's collectives and lax.ppermute only.
A program may use at most 256 MiB of HBM per device.

v0:
```python
import jax
import jax.numpy as jnp
from jax import lax
from jax.sharding import PartitionSpec as P

HEAD_DIM = 128
SEG = 512
RATE = 2
MROWS = 128
COMP = 256


def shifted(value, axis, by):
    size = lax.axis_size(axis)
    pairs = [(i, i + by) for i in range(size) if 0 <= i + by < size]
    return lax.ppermute(value, axis, pairs)


def standardize(values):
    centered = values - jnp.mean(values, -1, keepdims=True)
    variance = jnp.mean(centered * centered, -1, keepdims=True)
    return centered * lax.rsqrt(variance + 1e-05)


def matmul(left, right):
    return jnp.dot(left, right, preferred_element_type=jnp.float32)


def back_matmul(left, right):
    return jnp.einsum("smo,io->smi", left, right, preferred_element_type=jnp.float32)


def outer_sum(left, right):
    return jnp.einsum("smi,smo->io", left, right, preferred_element_type=jnp.float32)


def row_sum(values):
    return jnp.sum(values, axis=(0, 1))


def guarded_update(buffer, piece, start, axis, valid):
    current = lax.dynamic_slice_in_dim(buffer, start, piece.shape[axis], axis)
    return lax.dynamic_update_slice_in_dim(buffer, jnp.where(valid, piece, current), start, axis)


def body(
    inputs,
    memories,
    compressed,
    documents,
    cotangent,
    compressed_cotangent,
    query_weight,
    key_weight,
    value_weight,
    output_weight,
    output_bias,
    inner_weight,
    inner_bias,
    outer_weight,
    outer_bias,
    conv_weight,
    conv_bias,
    attn_gain,
    attn_shift,
    ffn_gain,
    ffn_shift,
):
    section = lax.axis_index("pipe")
    sections = lax.axis_size("pipe")
    segments, context = documents.shape
    width = inputs.shape[1]
    local = query_weight.shape[2]
    head_count = local // HEAD_DIM
    held = context - SEG
    blocks = SEG // MROWS
    ticks = blocks + sections - 1
    scale = HEAD_DIM ** (-0.5)
    query_w = query_weight[0]
    key_w = key_weight[0]
    value_w = value_weight[0]
    output_w = output_weight[0]
    inner_w = inner_weight[0]
    outer_w = outer_weight[0]
    output_b = output_bias[0].astype(jnp.float32)
    inner_b = inner_bias[0].astype(jnp.float32)
    outer_b = outer_bias[0].astype(jnp.float32)
    gain_a = attn_gain[0].astype(jnp.float32)
    shift_a = attn_shift[0].astype(jnp.float32)
    gain_f = ffn_gain[0].astype(jnp.float32)
    shift_f = ffn_shift[0].astype(jnp.float32)
    positions = jnp.arange(context, dtype=jnp.int32)
    memory_context = jnp.concatenate([compressed[0], memories[0]], 1).astype(jnp.float32)
    memory_hat = standardize(memory_context)
    memory_low = (memory_hat * gain_a + shift_a).astype(jnp.bfloat16)
    empty_rows = jnp.zeros((segments, SEG, local), jnp.bfloat16)
    key_buffer = jnp.concatenate([matmul(memory_low, key_w).astype(jnp.bfloat16), empty_rows], 1)
    value_buffer = jnp.concatenate(
        [matmul(memory_low, value_w).astype(jnp.bfloat16), empty_rows], 1
    )
    squeeze_rows = memories[0].reshape(segments, COMP, RATE * width)
    squeezed = matmul(squeeze_rows, conv_weight[0].reshape(RATE * width, local)) + conv_bias[
        0
    ].astype(jnp.float32)
    feature_start = lax.axis_index("tensor") * local
    kept_old = lax.dynamic_slice_in_dim(compressed[0][:, COMP:], feature_start, local, 2)
    new_compressed = jnp.concatenate([kept_old, squeezed.astype(jnp.bfloat16)], 1)[None]
    squeeze_cot = compressed_cotangent[0]
    conv_g = outer_sum(squeeze_rows, squeeze_cot).reshape(RATE, width, local)
    conv_bg = row_sum(squeeze_cot.astype(jnp.float32))

    def mask_for(start):
        query_docs = lax.dynamic_slice_in_dim(documents, held + start, MROWS, 1)
        query_pos = held + start + jnp.arange(MROWS, dtype=jnp.int32)
        return (positions[None, None, :] <= query_pos[None, :, None]) & (
            query_docs[:, :, None] == documents[:, None, :]
        )

    def project_queries(block_in):
        block_hat, hat_pull = jax.vjp(standardize, block_in)
        block_low = (block_hat * gain_a + shift_a).astype(jnp.bfloat16)
        queries = matmul(block_low, query_w).astype(jnp.bfloat16)
        return (block_hat, hat_pull, block_low, queries)

    def score_block(queries, keys, allowed):
        scores = (
            jnp.einsum(
                "sqhe,skhe->shqk",
                queries.reshape(segments, MROWS, head_count, HEAD_DIM),
                keys.reshape(segments, context, head_count, HEAD_DIM),
                preferred_element_type=jnp.float32,
            )
            * scale
        )
        return jnp.where(allowed[:, None], scores, -1e30)

    def finish_block(block_in, probs_low, values):
        mixed = jnp.einsum(
            "shqk,skhe->sqhe",
            probs_low,
            values.reshape(segments, context, head_count, HEAD_DIM),
            preferred_element_type=jnp.float32,
        )
        mixed = mixed.astype(jnp.bfloat16).reshape(segments, MROWS, local)
        attended = lax.psum(matmul(mixed, output_w), "tensor") + output_b
        hidden = block_in + attended
        hidden_hat, hidden_pull = jax.vjp(standardize, hidden)
        hidden_low = (hidden_hat * gain_f + shift_f).astype(jnp.bfloat16)
        pre = matmul(hidden_low, inner_w) + inner_b
        acts, gelu_pull = jax.vjp(jax.nn.gelu, pre)
        acts_low = acts.astype(jnp.bfloat16)
        branch = lax.psum(matmul(acts_low, outer_w), "tensor") + outer_b
        return (hidden + branch, (mixed, hidden_hat, hidden_pull, hidden_low, gelu_pull, acts_low))

    seg_inputs = inputs.reshape(segments, SEG, width).astype(jnp.float32)
    seg_cot = cotangent.reshape(segments, SEG, width).astype(jnp.float32)
    stored_inputs = jnp.zeros((segments, SEG, width), jnp.float32)
    stored_lse = jnp.zeros((segments, head_count, SEG), jnp.float32)
    layer_out = jnp.zeros((segments, SEG, width), jnp.float32)
    arriving = jnp.zeros((segments, MROWS, width), jnp.float32)
    for tick in range(ticks):
        block = tick - section
        valid = (block >= 0) & (block < blocks)
        start = jnp.clip(block, 0, blocks - 1) * MROWS
        block_in = jnp.where(
            section == 0, lax.dynamic_slice_in_dim(seg_inputs, start, MROWS, 1), arriving
        )
        block_hat, hat_pull, block_low, queries = project_queries(block_in)
        spot = held + start
        key_buffer = guarded_update(
            key_buffer, matmul(block_low, key_w).astype(jnp.bfloat16), spot, 1, valid
        )
        value_buffer = guarded_update(
            value_buffer, matmul(block_low, value_w).astype(jnp.bfloat16), spot, 1, valid
        )
        scores = score_block(queries, key_buffer, mask_for(start))
        top = jnp.max(scores, -1, keepdims=True)
        exps = jnp.exp(scores - top)
        total = jnp.sum(exps, -1, keepdims=True)
        probs_low = (exps / total).astype(jnp.bfloat16)
        block_lse = (top + jnp.log(total))[..., 0]
        block_out, unused = finish_block(block_in, probs_low, value_buffer)
        stored_inputs = guarded_update(stored_inputs, block_in, start, 1, valid)
        stored_lse = guarded_update(stored_lse, block_lse, start, 2, valid)
        layer_out = guarded_update(layer_out, block_out, start, 1, valid)
        if tick + 1 < ticks:
            arriving = shifted(block_out, "pipe", 1)
    key_grads = jnp.zeros((segments, context, local), jnp.float32)
    value_grads = jnp.zeros((segments, context, local), jnp.float32)
    query_g = jnp.zeros((width, local), jnp.float32)
    key_g = jnp.zeros((width, local), jnp.float32)
    value_g = jnp.zeros((width, local), jnp.float32)
    output_g = jnp.zeros((local, width), jnp.float32)
    output_bg = jnp.zeros((width,), jnp.float32)
    inner_g = jnp.zeros((width, inner_w.shape[1]), jnp.float32)
    inner_bg = jnp.zeros((inner_w.shape[1],), jnp.float32)
    outer_g = jnp.zeros((inner_w.shape[1], width), jnp.float32)
    outer_bg = jnp.zeros((width,), jnp.float32)
    gain_ag = jnp.zeros((width,), jnp.float32)
    shift_ag = jnp.zeros((width,), jnp.float32)
    gain_fg = jnp.zeros((width,), jnp.float32)
    shift_fg = jnp.zeros((width,), jnp.float32)
    input_grads = jnp.zeros((segments, SEG, width), jnp.float32)
    arriving_grad = jnp.zeros((segments, MROWS, width), jnp.float32)
    for tick in range(ticks):
        block = blocks - 1 - tick + (sections - 1 - section)
        valid = (block >= 0) & (block < blocks)
        keep = valid.astype(jnp.float32)
        start = jnp.clip(block, 0, blocks - 1) * MROWS
        grad_out = jnp.where(
            section == sections - 1,
            lax.dynamic_slice_in_dim(seg_cot, start, MROWS, 1),
            arriving_grad,
        )
        block_in = lax.dynamic_slice_in_dim(stored_inputs, start, MROWS, 1)
        block_lse = lax.dynamic_slice_in_dim(stored_lse, start, MROWS, 2)
        block_hat, hat_pull, block_low, queries = project_queries(block_in)
        scores = score_block(queries, key_buffer, mask_for(start))
        probs = jnp.exp(scores - block_lse[..., None])
        probs_low = probs.astype(jnp.bfloat16)
        unused, kept = finish_block(block_in, probs_low, value_buffer)
        mixed, hidden_hat, hidden_pull, hidden_low, gelu_pull, acts_low = kept
        branch_grad = grad_out.astype(jnp.bfloat16)
        outer_bg = outer_bg + keep * row_sum(branch_grad.astype(jnp.float32))
        outer_g = outer_g + keep * outer_sum(acts_low, branch_grad)
        pre_grad = gelu_pull(back_matmul(branch_grad, outer_w))[0].astype(jnp.bfloat16)
        inner_bg = inner_bg + keep * row_sum(pre_grad.astype(jnp.float32))
        inner_g = inner_g + keep * outer_sum(hidden_low, pre_grad)
        normed_part = back_matmul(pre_grad, inner_w)
        gain_fg = gain_fg + keep * row_sum(normed_part * hidden_hat)
        shift_fg = shift_fg + keep * row_sum(normed_part)
        normed_grad = lax.psum(normed_part, "tensor")
        hidden_grad = grad_out + hidden_pull(normed_grad * gain_f)[0]
        attend_grad = hidden_grad.astype(jnp.bfloat16)
        output_bg = output_bg + keep * row_sum(attend_grad.astype(jnp.float32))
        output_g = output_g + keep * outer_sum(mixed, attend_grad)
        mixed_grad = (
            back_matmul(attend_grad, output_w)
            .astype(jnp.bfloat16)
            .reshape(segments, MROWS, head_count, HEAD_DIM)
        )
        values_split = value_buffer.reshape(segments, context, head_count, HEAD_DIM)
        keys_split = key_buffer.reshape(segments, context, head_count, HEAD_DIM)
        queries_split = queries.reshape(segments, MROWS, head_count, HEAD_DIM)
        probs_grad = jnp.einsum(
            "sqhe,skhe->shqk", mixed_grad, values_split, preferred_element_type=jnp.float32
        )
        score_grad = (probs * (probs_grad - jnp.sum(probs * probs_grad, -1, keepdims=True))).astype(
            jnp.bfloat16
        )
        query_rows = (
            (
                jnp.einsum(
                    "shqk,skhe->sqhe", score_grad, keys_split, preferred_element_type=jnp.float32
                )
                * scale
            )
            .astype(jnp.bfloat16)
            .reshape(segments, MROWS, local)
        )
        key_add = (
            jnp.einsum(
                "shqk,sqhe->skhe", score_grad, queries_split, preferred_element_type=jnp.float32
            )
            * scale
        )
        value_add = jnp.einsum(
            "shqk,sqhe->skhe", probs_low, mixed_grad, preferred_element_type=jnp.float32
        )
        key_grads = key_grads + keep * key_add.reshape(segments, context, local)
        value_grads = value_grads + keep * value_add.reshape(segments, context, local)
        spot = held + start
        block_kg = lax.dynamic_slice_in_dim(key_grads, spot, MROWS, 1).astype(jnp.bfloat16)
        block_vg = lax.dynamic_slice_in_dim(value_grads, spot, MROWS, 1).astype(jnp.bfloat16)
        query_g = query_g + keep * outer_sum(block_low, query_rows)
        key_g = key_g + keep * outer_sum(block_low, block_kg)
        value_g = value_g + keep * outer_sum(block_low, block_vg)
        normed_att = (
            back_matmul(query_rows, query_w)
            + back_matmul(block_kg, key_w)
            + back_matmul(block_vg, value_w)
        )
        gain_ag = gain_ag + keep * row_sum(normed_att * block_hat)
        shift_ag = shift_ag + keep * row_sum(normed_att)
        normed_full = lax.psum(normed_att, "tensor")
        block_grad = hidden_grad + hat_pull(normed_full * gain_a)[0]
        input_grads = guarded_update(input_grads, block_grad, start, 1, valid)
        if tick + 1 < ticks:
            arriving_grad = shifted(block_grad, "pipe", -1)
    memory_kg = key_grads[:, :held].astype(jnp.bfloat16)
    memory_vg = value_grads[:, :held].astype(jnp.bfloat16)
    key_g = key_g + outer_sum(memory_low, memory_kg)
    value_g = value_g + outer_sum(memory_low, memory_vg)
    memory_part = back_matmul(memory_kg, key_w) + back_matmul(memory_vg, value_w)
    gain_ag = gain_ag + row_sum(memory_part * memory_hat)
    shift_ag = shift_ag + row_sum(memory_part)
    gain_ag, shift_ag, gain_fg, shift_fg = lax.psum(
        (gain_ag, shift_ag, gain_fg, shift_fg), ("dp", "tensor")
    )
    (
        query_g,
        key_g,
        value_g,
        output_g,
        output_bg,
        inner_g,
        inner_bg,
        outer_g,
        outer_bg,
        conv_g,
        conv_bg,
    ) = lax.psum(
        (
            query_g,
            key_g,
            value_g,
            output_g,
            output_bg,
            inner_g,
            inner_bg,
            outer_g,
            outer_bg,
            conv_g,
            conv_bg,
        ),
        "dp",
    )
    return (
        layer_out.reshape(segments * SEG, width)[None],
        new_compressed,
        input_grads.reshape(segments * SEG, width)[None],
        query_g[None],
        key_g[None],
        value_g[None],
        output_g[None],
        output_bg[None],
        inner_g[None],
        inner_bg[None],
        outer_g[None],
        outer_bg[None],
        conv_g[None],
        conv_bg[None],
        gain_ag[None],
        shift_ag[None],
        gain_fg[None],
        shift_fg[None],
    )


def solution(mesh):
    return jax.shard_map(
        body,
        mesh=mesh,
        in_specs=(
            P("dp", None),
            P("pipe", "dp", None, None),
            P("pipe", "dp", None, None),
            P("dp", None),
            P("dp", None),
            P("pipe", "dp", None, "tensor"),
            P("pipe", None, "tensor"),
            P("pipe", None, "tensor"),
            P("pipe", None, "tensor"),
            P("pipe", "tensor", None),
            P("pipe", None),
            P("pipe", None, "tensor"),
            P("pipe", "tensor"),
            P("pipe", "tensor", None),
            P("pipe", None),
            P("pipe", None, None, "tensor"),
            P("pipe", "tensor"),
            P("pipe", None),
            P("pipe", None),
            P("pipe", None),
            P("pipe", None),
        ),
        out_specs=(
            P("pipe", "dp", None),
            P("pipe", "dp", None, "tensor"),
            P("pipe", "dp", None),
            P("pipe", None, "tensor"),
            P("pipe", None, "tensor"),
            P("pipe", None, "tensor"),
            P("pipe", "tensor", None),
            P("pipe", None),
            P("pipe", None, "tensor"),
            P("pipe", "tensor"),
            P("pipe", "tensor", None),
            P("pipe", None),
            P("pipe", None, None, "tensor"),
            P("pipe", "tensor"),
            P("pipe", None),
            P("pipe", None),
            P("pipe", None),
            P("pipe", None),
        ),
        check_vma=False,
    )
```

profile of v0, /device:TPU:0, one launch (start us, length us, event | category | flops | bytes accessed | tf_op | source)
XLA Modules:
  0.0 1610.5 jit_solution(14114041018935914976)
XLA Ops:
  35.8 40.0 %all-reduce.32.cloned.1.call-done = f32[1,128,1024]{2,1,0:T(8,128)} async-done(((f32[1,128,1024]{2,1,0:T(8,128)}), f32[1,128,1024]{2,1,0:T(8,128)}) %all-reduce.32.cloned.1.call-update) | async-done | bytes 524304 | tf_op jit(solution)/shard_map/psum | solution.py:145
  80.4 3.5 fusion.101
  84.0 38.6 %all-reduce.34.cloned.1.call-done = f32[1,128,1024]{2,1,0:T(8,128)} async-done(((f32[1,128,1024]{2,1,0:T(8,128)}), f32[1,128,1024]{2,1,0:T(8,128)}) %all-reduce.34.cloned.1.call-update) | async-done | bytes 524304 | tf_op jit(solution)/shard_map/psum | solution.py:152
  125.3 5.4 collective-permute-start
  130.7 11.2 collective-permute-done
  157.0 39.8 %all-reduce.36.cloned.1.call-done = f32[1,128,1024]{2,1,0:T(8,128)} async-done(((f32[1,128,1024]{2,1,0:T(8,128)}), f32[1,128,1024]{2,1,0:T(8,128)}) %all-reduce.36.cloned.1.call-update) | async-done | bytes 524304 | tf_op jit(solution)/shard_map/psum | solution.py:145
  199.2 3.5 fusion.104
  202.7 38.7 %all-reduce.38.cloned.1.call-done = f32[1,128,1024]{2,1,0:T(8,128)} async-done(((f32[1,128,1024]{2,1,0:T(8,128)}), f32[1,128,1024]{2,1,0:T(8,128)}) %all-reduce.38.cloned.1.call-update) | async-done | bytes 524304 | tf_op jit(solution)/shard_map/psum | solution.py:152
  243.9 5.4 collective-permute-start.1
  249.3 11.2 collective-permute-done.1
  275.5 40.1 %all-reduce.40.cloned.1.call-done = f32[1,128,1024]{2,1,0:T(8,128)} async-done(((f32[1,128,1024]{2,1,0:T(8,128)}), f32[1,128,1024]{2,1,0:T(8,128)}) %all-reduce.40.cloned.1.call-update) | async-done | bytes 524304 | tf_op jit(solution)/shard_map/psum | solution.py:145
  317.9 3.5 fusion.107
  321.4 38.6 %all-reduce.42.cloned.1.call-done = f32[1,128,1024]{2,1,0:T(8,128)} async-done(((f32[1,128,1024]{2,1,0:T(8,128)}), f32[1,128,1024]{2,1,0:T(8,128)}) %all-reduce.42.cloned.1.call-update) | async-done | bytes 524304 | tf_op jit(solution)/shard_map/psum | solution.py:152
  362.5 5.4 collective-permute-start.2
  367.9 11.2 collective-permute-done.2
  394.1 40.0 %all-reduce.44.cloned.1.call-done = f32[1,128,1024]{2,1,0:T(8,128)} async-done(((f32[1,128,1024]{2,1,0:T(8,128)}), f32[1,128,1024]{2,1,0:T(8,128)}) %all-reduce.44.cloned.1.call-update) | async-done | bytes 524304 | tf_op jit(solution)/shard_map/psum | solution.py:145
  436.5 3.5 fusion.110
  449.7 3.0 convolution_bitcast_fusion
  452.8 25.9 %all-reduce.46.cloned.1.call-done = f32[1,128,1024]{2,1,0:T(8,128)} async-done(((f32[1,128,1024]{2,1,0:T(8,128)}), f32[1,128,1024]{2,1,0:T(8,128)}) %all-reduce.46.cloned.1.call-update) | async-done | bytes 524304 | tf_op jit(solution)/shard_map/psum | solution.py:152
  481.0 5.0 collective-permute-start.3
  486.1 11.1 collective-permute-done.3
  526.7 37.0 %all-reduce.48.cloned.1.call-done = f32[1,128,1024]{2,1,0:T(8,128)} async-done(((f32[1,128,1024]{2,1,0:T(8,128)}), f32[1,128,1024]{2,1,0:T(8,128)}) %all-reduce.48.cloned.1.call-update) | async-done | bytes 524304 | tf_op jit(solution)/shard_map/psum | solution.py:145
  571.8 3.9 fusion.411
  575.8 2.9 fusion.673
  578.6 31.8 %all-reduce.50.cloned.1.call-done = f32[1,128,1024]{2,1,0:T(8,128)} async-done(((f32[1,128,1024]{2,1,0:T(8,128)}), f32[1,128,1024]{2,1,0:T(8,128)}) %all-reduce.50.cloned.1.call-update) | async-done | bytes 524304 | tf_op jit(solution)/shard_map/psum | solution.py:232
  633.2 32.7 %all-reduce.52.cloned.1.call-done = f32[1,128,1024]{2,1,0:T(8,128)} async-done(((f32[1,128,1024]{2,1,0:T(8,128)}), f32[1,128,1024]{2,1,0:T(8,128)}) %all-reduce.52.cloned.1.call-update) | async-done | bytes 524304 | tf_op jit(solution)/shard_map/psum | solution.py:285
  665.9 3.1 multiply_reduce_fusion.15
  700.0 23.6 %all-reduce.54.cloned.1.call-done = f32[1,128,1024]{2,1,0:T(8,128)} async-done(((f32[1,128,1024]{2,1,0:T(8,128)}), f32[1,128,1024]{2,1,0:T(8,128)}) %all-reduce.54.cloned.1.call-update) | async-done | bytes 524304 | tf_op jit(solution)/shard_map/psum | solution.py:145
  730.0 15.5 collective-permute-done.4
  752.8 4.0 fusion.412
  759.5 29.6 %all-reduce.56.cloned.1.call-done = f32[1,128,1024]{2,1,0:T(8,128)} async-done(((f32[1,128,1024]{2,1,0:T(8,128)}), f32[1,128,1024]{2,1,0:T(8,128)}) %all-reduce.56.cloned.1.call-update) | async-done | bytes 524304 | tf_op jit(solution)/shard_map/psum | solution.py:232
  816.1 34.6 %all-reduce.72.cloned.1.call-done = (f32[1,128,1024]{2,1,0:T(8,128)}, f32[1,128,1024]{2,1,0:T(8,128)}) async-done(((f32[1,128,1024]{2,1,0:T(8,128)}, f32[1,128,1024]{2,1,0:T(8,128)}), (f32[1,128,1024]{2,1,0:T(8,128)}, f32[1,128,1024]{2,1,0:T(8,128)})) %all-reduce.72.cloned.1.call-update) | async-done | bytes 1048592 | tf_op jit(solution)/shard_map/psum | solution.py:285
  858.9 15.3 collective-permute-done.5
  881.6 3.9 fusion.413
  888.4 30.0 %all-reduce.58.cloned.1.call-done = f32[1,128,1024]{2,1,0:T(8,128)} async-done(((f32[1,128,1024]{2,1,0:T(8,128)}), f32[1,128,1024]{2,1,0:T(8,128)}) %all-reduce.58.cloned.1.call-update) | async-done | bytes 524304 | tf_op jit(solution)/shard_map/psum | solution.py:232
  945.2 34.7 %all-reduce.70.cloned.1.call-done = (f32[1,128,1024]{2,1,0:T(8,128)}, f32[1,128,1024]{2,1,0:T(8,128)}) async-done(((f32[1,128,1024]{2,1,0:T(8,128)}, f32[1,128,1024]{2,1,0:T(8,128)}), (f32[1,128,1024]{2,1,0:T(8,128)}, f32[1,128,1024]{2,1,0:T(8,128)})) %all-reduce.70.cloned.1.call-update) | async-done | bytes 1048592 | tf_op jit(solution)/shard_map/psum | solution.py:285
  988.1 15.3 collective-permute-done.6
  1011.1 4.0 fusion.414
  1017.9 29.7 %all-reduce.60.cloned.1.call-done = f32[1,128,1024]{2,1,0:T(8,128)} async-done(((f32[1,128,1024]{2,1,0:T(8,128)}), f32[1,128,1024]{2,1,0:T(8,128)}) %all-reduce.60.cloned.1.call-update) | async-done | bytes 524304 | tf_op jit(solution)/shard_map/psum | solution.py:232
  1074.5 34.7 %all-reduce.68.cloned.1.call-done = (f32[1,128,1024]{2,1,0:T(8,128)}, f32[1,128,1024]{2,1,0:T(8,128)}) async-done(((f32[1,128,1024]{2,1,0:T(8,128)}, f32[1,128,1024]{2,1,0:T(8,128)}), (f32[1,128,1024]{2,1,0:T(8,128)}, f32[1,128,1024]{2,1,0:T(8,128)})) %all-reduce.68.cloned.1.call-update) | async-done | bytes 1048592 | tf_op jit(solution)/shard_map/psum | solution.py:285
  1117.5 15.3 collective-permute-done.7
  1140.2 9.9 add_bitcast_fusion.1
  1152.9 3.6 add_bitcast_fusion
  1156.5 24.5 %all-reduce.66.cloned.1.call-done = (f32[1,128,1024]{2,1,0:T(8,128)}, f32[1,128,1024]{2,1,0:T(8,128)}) async-done(((f32[1,128,1024]{2,1,0:T(8,128)}, f32[1,128,1024]{2,1,0:T(8,128)}), (f32[1,128,1024]{2,1,0:T(8,128)}, f32[1,128,1024]{2,1,0:T(8,128)})) %all-reduce.66.cloned.1.call-update) | async-done | bytes 1048592 | tf_op jit(solution)/shard_map/psum | solution.py:145
  1189.0 3.3 multiply_reduce_fusion.1
  1195.5 3.3 fusion.113
  1223.8 76.1 %all-reduce.3 = (f32[1,1024]{1,0:T(1,128)}, f32[1,1024]{1,0:T(1,128)}, f32[1,1024]{1,0:T(1,128)}, f32[1,256]{1,0:T(1,128)}) all-reduce(f32[1,1024]{1,0:T(1,128)S(1)} %bitcast.1179, f32[1,1024]{1,0:T(1,128)S(1)} %bitcast.1176, f32[1,1024]{1,0:T(1,128)S(1)} %bitcast.1175, ...), channel_id=1, replica_groups=mesh['pipe'=2,'dp'=16,'tensor'=4] {'dp'}, use_global_device_ids=true, to_apply=%region_111.112 | all-reduce | flops 3328 | bytes 26624 | tf_op jit(solution)/shard_map/psum | solution.py:312
  1306.5 277.8 %all-reduce.2 = (f32[1,1024]{1,0:T(1,128)}, f32[1,1024]{1,0:T(1,128)}, f32[1,1024]{1,0:T(1,128)}, f32[1,1024]{1,0:T(1,128)}) all-reduce(f32[1,1024]{1,0:T(1,128)S(1)} %bitcast.1178, f32[1,1024]{1,0:T(1,128)S(1)} %bitcast.1177, f32[1,1024]{1,0:T(1,128)S(1)} %bitcast.1181, ...), channel_id=1, replica_groups=mesh['pipe'=2,'dp'=16,'tensor'=4] {'dp','tensor'}, use_global_device_ids=true, to_apply=%region_135.136 | all-reduce | flops 4096 | bytes 32768 | tf_op jit(solution)/shard_map/psum | solution.py:297
  (987 shorter events, 407.6 us)
Async XLA Ops:
  7.2 73.2 %copy-start = (bf16[1,1024,1024]{2,1,0:T(8,128)(2,1)S(1)}, bf16[1,1024,1024]{2,1,0:T(8,128)(2,1)}, u32[]{:S(2)}) copy-start(bf16[1,1024,1024]{2,1,0:T(8,128)(2,1)} %param.32) | copy-start | bytes 6291460
  7.2 68.6 %all-reduce.32.cloned.1.call-start = ((), (), s32[]{:S(2)}) async-start(), calls=%async_computation | async-start | bytes 1048576 | tf_op jit(solution)/shard_map/psum | solution.py:145
  9.0 496.8 %copy-start.196 = (f32[1,1024]{1,0:T(1,128)}, f32[1,1024]{1,0:T(1,128)S(1)}, u32[]{:S(2)}) copy-start(f32[1,1024]{1,0:T(1,128)S(1)} %convert_element_type.921) | copy-start | bytes 12292
  30.7 121.4 %copy-start.162 = (pred[128,1536]{1,0:T(8,128)(4,1)}, pred[128,1536]{1,0:T(8,128)(4,1)S(1)}, u32[]{:S(2)}) copy-start(pred[128,1536]{1,0:T(8,128)(4,1)S(1)} %get-tuple-element.174) | copy-start | bytes 589828
  35.7 86.9 %all-reduce.34.cloned.1.call-start = ((), (), s32[]{:S(2)}) async-start(), calls=%async_computation.1 | async-start | bytes 1048576 | tf_op jit(solution)/shard_map/psum | solution.py:152
  35.8 400.7 %copy-start.200 = (f32[1,1024]{1,0:T(1,128)}, f32[1,1024]{1,0:T(1,128)S(1)}, u32[]{:S(2)}) copy-start(f32[1,1024]{1,0:T(1,128)S(1)} %convert_element_type.925) | copy-start | bytes 12292
  83.9 112.9 %all-reduce.36.cloned.1.call-start = ((), (), s32[]{:S(2)}) async-start(), calls=%async_computation.2 | async-start | bytes 1048576 | tf_op jit(solution)/shard_map/psum | solution.py:145
  84.0 394.7 %copy-start.198 = (f32[1,1024]{1,0:T(1,128)}, f32[1,1024]{1,0:T(1,128)S(1)}, u32[]{:S(2)}) copy-start(f32[1,1024]{1,0:T(1,128)S(1)} %convert_element_type.926) | copy-start | bytes 12292
  125.3 16.6 %collective-permute-start = (f32[1,128,1024]{2,1,0:T(8,128)}, f32[1,128,1024]{2,1,0:T(8,128)}, u32[]{:S(2)}, u32[]{:S(2)}) collective-permute-start(f32[1,128,1024]{2,1,0:T(8,128)} %get-tuple-element.155), channel_id=1, source_target_pairs={{0,64},{1,65},{2,66},{3,67},{4,68},{5,69},{6,70},{7,71},{8,72},{9,... | collective-permute-start | bytes 1572872 | tf_op jit(solution)/shard_map/ppermute | solution.py:16
  156.8 84.6 %all-reduce.38.cloned.1.call-start = ((), (), s32[]{:S(2)}) async-start(), calls=%async_computation.3 | async-start | bytes 1048576 | tf_op jit(solution)/shard_map/psum | solution.py:152
  202.7 112.9 %all-reduce.40.cloned.1.call-start = ((), (), s32[]{:S(2)}) async-start(), calls=%async_computation.4 | async-start | bytes 1048576 | tf_op jit(solution)/shard_map/psum | solution.py:145
  243.9 16.6 %collective-permute-start.1 = (f32[1,128,1024]{2,1,0:T(8,128)}, f32[1,128,1024]{2,1,0:T(8,128)}, u32[]{:S(2)}, u32[]{:S(2)}) collective-permute-start(f32[1,128,1024]{2,1,0:T(8,128)} %get-tuple-element.151), channel_id=1, source_target_pairs={{0,64},{1,65},{2,66},{3,67},{4,68},{5,69},{6,70},{7,71},{8,72},{9,... | collective-permute-start | bytes 1572872 | tf_op jit(solution)/shard_map/ppermute | solution.py:16
  275.4 84.6 %all-reduce.42.cloned.1.call-start = ((), (), s32[]{:S(2)}) async-start(), calls=%async_computation.5 | async-start | bytes 1048576 | tf_op jit(solution)/shard_map/psum | solution.py:152
  321.4 112.8 %all-reduce.44.cloned.1.call-start = ((), (), s32[]{:S(2)}) async-start(), calls=%async_computation.6 | async-start | bytes 1048576 | tf_op jit(solution)/shard_map/psum | solution.py:145
  362.5 16.6 %collective-permute-start.2 = (f32[1,128,1024]{2,1,0:T(8,128)}, f32[1,128,1024]{2,1,0:T(8,128)}, u32[]{:S(2)}, u32[]{:S(2)}) collective-permute-start(f32[1,128,1024]{2,1,0:T(8,128)} %get-tuple-element.147), channel_id=1, source_target_pairs={{0,64},{1,65},{2,66},{3,67},{4,68},{5,69},{6,70},{7,71},{8,72},{9,... | collective-permute-start | bytes 1572872 | tf_op jit(solution)/shard_map/ppermute | solution.py:16
  394.1 84.6 %all-reduce.46.cloned.1.call-start = ((), (), s32[]{:S(2)}) async-start(), calls=%async_computation.7 | async-start | bytes 1048576 | tf_op jit(solution)/shard_map/psum | solution.py:152
  440.0 123.7 %all-reduce.48.cloned.1.call-start = ((), (), s32[]{:S(2)}) async-start(), calls=%async_computation.8 | async-start | bytes 1048576 | tf_op jit(solution)/shard_map/psum | solution.py:145
  481.0 16.2 %collective-permute-start.3 = (f32[1,128,1024]{2,1,0:T(8,128)S(1)}, f32[1,128,1024]{2,1,0:T(8,128)S(1)}, u32[]{:S(2)}, u32[]{:S(2)}) collective-permute-start(f32[1,128,1024]{2,1,0:T(8,128)S(1)} %get-tuple-element.143), channel_id=1, source_target_pairs={{0,64},{1,65},{2,66},{3,67},{4,68},{5,69},{6,70},{7,71},{8,72},{9,... | collective-permute-start | bytes 1572872 | tf_op jit(solution)/shard_map/ppermute | solution.py:16
  523.7 86.7 %all-reduce.50.cloned.1.call-start = ((), (), s32[]{:S(2)}) async-start(), calls=%async_computation.9 | async-start | bytes 1048576 | tf_op jit(solution)/shard_map/psum | solution.py:232
  523.8 41.5 %copy-start.201 = (f32[1,1024]{1,0:T(1,128)S(1)}, f32[1,1024]{1,0:T(1,128)}, u32[]{:S(2)}) copy-start(f32[1,1024]{1,0:T(1,128)} %copy-done.200) | copy-start | bytes 12292
  571.8 94.2 %all-reduce.52.cloned.1.call-start = ((), (), s32[]{:S(2)}) async-start(), calls=%async_computation.10 | async-start | bytes 1048576 | tf_op jit(solution)/shard_map/psum | solution.py:285
  627.2 96.4 %all-reduce.54.cloned.1.call-start = ((), (), s32[]{:S(2)}) async-start(), calls=%async_computation.11 | async-start | bytes 1048576 | tf_op jit(solution)/shard_map/psum | solution.py:145
  684.8 104.3 %all-reduce.56.cloned.1.call-start = ((), (), s32[]{:S(2)}) async-start(), calls=%async_computation.12 | async-start | bytes 1048576 | tf_op jit(solution)/shard_map/psum | solution.py:232
  727.9 17.6 %collective-permute-start.4 = (f32[1,128,1024]{2,1,0:T(8,128)S(1)}, f32[1,128,1024]{2,1,0:T(8,128)S(1)}, u32[]{:S(2)}, u32[]{:S(2)}) collective-permute-start(f32[1,128,1024]{2,1,0:T(8,128)S(1)} %get-tuple-element.103), channel_id=1, source_target_pairs={{64,0},{65,1},{66,2},{67,3},{68,4},{69,5},{70,6},{71,7},{72,8},{73... | collective-permute-start | bytes 1572872 | tf_op jit(solution)/shard_map/ppermute | solution.py:16
  752.5 98.1 %all-reduce.72.cloned.1.call-start = ((), (), s32[]{:S(2)}) async-start(), calls=%async_computation.20 | async-start | bytes 2097152 | tf_op jit(solution)/shard_map/psum | solution.py:285
  807.8 110.5 %all-reduce.58.cloned.1.call-start = ((), (), s32[]{:S(2)}) async-start(), calls=%async_computation.13 | async-start | bytes 1048576 | tf_op jit(solution)/shard_map/psum | solution.py:232
  856.8 17.4 %collective-permute-start.5 = (f32[1,128,1024]{2,1,0:T(8,128)S(1)}, f32[1,128,1024]{2,1,0:T(8,128)S(1)}, u32[]{:S(2)}, u32[]{:S(2)}) collective-permute-start(f32[1,128,1024]{2,1,0:T(8,128)S(1)} %get-tuple-element.101), channel_id=1, source_target_pairs={{64,0},{65,1},{66,2},{67,3},{68,4},{69,5},{70,6},{71,7},{72,8},{73... | collective-permute-start | bytes 1572872 | tf_op jit(solution)/shard_map/ppermute | solution.py:16
  881.3 98.6 %all-reduce.70.cloned.1.call-start = ((), (), s32[]{:S(2)}) async-start(), calls=%async_computation.19 | async-start | bytes 2097152 | tf_op jit(solution)/shard_map/psum | solution.py:285
  937.1 110.5 %all-reduce.60.cloned.1.call-start = ((), (), s32[]{:S(2)}) async-start(), calls=%async_computation.14 | async-start | bytes 1048576 | tf_op jit(solution)/shard_map/psum | solution.py:232
  945.2 37.0 %copy-start.247 = (f32[128]{0:T(128)S(1)}, f32[128]{0:T(128)}, u32[]{:S(2)}) copy-start(f32[128]{0:T(128)} %broadcast_multiply_fusion.6) | copy-start | bytes 1540
  945.2 37.0 %copy-start.257 = (f32[128]{0:T(128)S(1)}, f32[128]{0:T(128)}, u32[]{:S(2)}) copy-start(f32[128]{0:T(128)} %copy-done.256) | copy-start | bytes 1540
  986.1 17.4 %collective-permute-start.6 = (f32[1,128,1024]{2,1,0:T(8,128)S(1)}, f32[1,128,1024]{2,1,0:T(8,128)S(1)}, u32[]{:S(2)}, u32[]{:S(2)}) collective-permute-start(f32[1,128,1024]{2,1,0:T(8,128)S(1)} %get-tuple-element.99), channel_id=1, source_target_pairs={{64,0},{65,1},{66,2},{67,3},{68,4},{69,5},{70,6},{71,7},{72,8},{73... | collective-permute-start | bytes 1572872 | tf_op jit(solution)/shard_map/ppermute | solution.py:16
  1010.6 98.6 %all-reduce.68.cloned.1.call-start = ((), (), s32[]{:S(2)}) async-start(), calls=%async_computation.18 | async-start | bytes 2097152 | tf_op jit(solution)/shard_map/psum | solution.py:285
  1066.4 114.6 %all-reduce.66.cloned.1.call-start = ((), (), s32[]{:S(2)}) async-start(), calls=%async_computation.17 | async-start | bytes 2097152 | tf_op jit(solution)/shard_map/psum | solution.py:145
  1074.5 37.1 %copy-start.278 = (f32[128]{0:T(128)S(1)}, f32[128]{0:T(128)}, u32[]{:S(2)}) copy-start(f32[128]{0:T(128)} %copy-done.277) | copy-start | bytes 1540
  1074.5 37.1 %copy-start.245 = (f32[128]{0:T(128)S(1)}, f32[128]{0:T(128)}, u32[]{:S(2)}) copy-start(f32[128]{0:T(128)} %broadcast_multiply_fusion.4) | copy-start | bytes 1540
  1074.5 37.1 %copy-start.255 = (f32[128]{0:T(128)S(1)}, f32[128]{0:T(128)}, u32[]{:S(2)}) copy-start(f32[128]{0:T(128)} %copy-done.254) | copy-start | bytes 1540
  1115.4 17.4 %collective-permute-start.7 = (f32[1,128,1024]{2,1,0:T(8,128)S(1)}, f32[1,128,1024]{2,1,0:T(8,128)S(1)}, u32[]{:S(2)}, u32[]{:S(2)}) collective-permute-start(f32[1,128,1024]{2,1,0:T(8,128)S(1)} %get-tuple-element.97), channel_id=1, source_target_pairs={{64,0},{65,1},{66,2},{67,3},{68,4},{69,5},{70,6},{71,7},{72,8},{73... | collective-permute-start | bytes 1572872 | tf_op jit(solution)/shard_map/ppermute | solution.py:16
  1139.9 164.7 %all-reduce.64.cloned.1.call-start = ((), (), s32[]{:S(2)}) async-start(), calls=%async_computation.16 | async-start | bytes 2097152 | tf_op jit(solution)/shard_map/psum | solution.py:152
  1208.2 381.6 %all-reduce.62.cloned.1.call-start = ((), (), s32[]{:S(2)}) async-start(), calls=%async_computation.15 | async-start | bytes 29360128 | tf_op jit(solution)/shard_map/psum | solution.py:312
  1220.7 79.2 %copy-start.224 = (f32[1024]{0:T(1024)S(1)}, f32[1024]{0:T(1024)}, u32[]{:S(2)}) copy-start(f32[1024]{0:T(1024)} %get-tuple-element.39) | copy-start | bytes 12292
  1220.7 79.2 %copy-start.227 = (f32[1024]{0:T(1024)S(1)}, f32[1024]{0:T(1024)}, u32[]{:S(2)}) copy-start(f32[1024]{0:T(1024)} %get-tuple-element.41) | copy-start | bytes 12292
  1220.7 79.2 %copy-start.230 = (f32[1024]{0:T(1024)S(1)}, f32[1024]{0:T(1024)}, u32[]{:S(2)}) copy-start(f32[1024]{0:T(1024)} %get-tuple-element.43) | copy-start | bytes 12292
  1220.8 79.2 %copy-start.233 = (f32[1024]{0:T(1024)S(1)}, f32[1024]{0:T(1024)}, u32[]{:S(2)}) copy-start(f32[1024]{0:T(1024)} %get-tuple-element.45) | copy-start | bytes 12292
  1220.8 79.2 %copy-start.236 = (f32[1024]{0:T(1024)S(1)}, f32[1024]{0:T(1024)}, u32[]{:S(2)}) copy-start(f32[1024]{0:T(1024)} %get-tuple-element.47) | copy-start | bytes 12292
  1304.5 279.8 %copy-start.276 = (f32[128]{0:T(128)S(1)}, f32[128]{0:T(128)}, u32[]{:S(2)}) copy-start(f32[128]{0:T(128)} %copy-done.275) | copy-start | bytes 1540
  1304.6 279.7 %copy-start.114 = (f32[1,128,1024]{2,1,0:T(8,128)S(1)}, f32[1,128,1024]{2,1,0:T(8,128)}, u32[]{:S(2)}) copy-start(f32[1,128,1024]{2,1,0:T(8,128)} %get-tuple-element.65) | copy-start | bytes 1572868
  1304.7 281.1 %copy-start.58 = (f32[1,128,1024]{2,1,0:T(8,128)S(1)}, f32[1,128,1024]{2,1,0:T(8,128)}, u32[]{:S(2)}) copy-start(f32[1,128,1024]{2,1,0:T(8,128)} %copy-done.56) | copy-start | bytes 1572868
  (275 other events, 1199.6 us)
Sparse Core Ops, SparseCore 0:
  35.8 40.0 all-reduce.31
  84.0 38.5 all-reduce.33
  156.9 39.8 all-reduce.35
  202.8 38.5 all-reduce.37
  275.5 39.9 all-reduce.39
  321.5 38.4 all-reduce.41
  394.2 39.9 all-reduce.43
  440.1 38.5 all-reduce.45
  523.8 39.8 all-reduce.47
  571.9 38.5 all-reduce.49
  627.3 38.5 all-reduce.51
  685.0 38.5 all-reduce.53
  752.7 36.4 all-reduce.55
  808.0 42.6 all-reduce.71
  881.4 36.8 all-reduce.57
  937.3 42.5 all-reduce.69
  1010.7 36.8 all-reduce.59
  1066.5 42.6 all-reduce.67
  1140.0 40.9 all-reduce.65
  1208.3 42.4 all-reduce.63
  1258.2 203.5 all-reduce.61
where the time goes:
time: 1620 us; the launch traced here: 1610 us
  waiting for transfers between devices  751 us (46%)
  blocking collectives  354 us (22%)
  matrix products  244 us (15%)
  other arithmetic  140 us (9%)
  local copies, waits for them, and re-layouts  74.3 us (5%)
  starting transfers between devices  28.6 us (2%)
  between operations  18.4 us (1%)
    psum x1, blocking collectives, body(): lax.psum((gain_ag, shift_ag, gain_fg, shift_fg), ('dp', 'tensor'))  278 us
    psum x7, waiting for transfers between devices, finish_block(): attended = lax.psum(matmul(mixed, output_w), 'tensor') + output_b  245 us
    psum x5, waiting for transfers between devices, finish_block(): branch = lax.psum(matmul(acts_low, outer_w), 'tensor') + outer_b  142 us
    psum x4, waiting for transfers between devices, body(): normed_full = lax.psum(normed_att, 'tensor')  137 us
    psum x4, waiting for transfers between devices, body(): normed_grad = lax.psum(normed_part, 'tensor')  121 us
    ppermute x8, waiting for transfers between devices, shifted(): return lax.ppermute(value, axis, pairs)  106 us
    dot_general x33, matrix products, outer_sum(): jnp.einsum('smi,smo->io', left, right, preferred_element_type=jnp.float32)  83.8 us
    psum x1, blocking collectives, body(): lax.psum((query_g, key_g, value_g, output_g, output_bg, inner_g, inner_bg...  76.1 us
  transfers between devices with their start and end apart: 29, of which 27 were waited for; matrix products, arithmetic and copies ran while one was open for 8% of the time, Pallas kernels for 0%

commit v1 on v0

v1 whole, which is shorter than its diff:
```python
import jax
import jax.numpy as jnp
from jax import lax
from jax.sharding import PartitionSpec as P

HEAD_DIM = 128
SEG = 512
RATE = 2
COMP = 256
AXES = ("pipe", "dp", "tensor")


def pairs(move):
    found = []
    for p in range(2):
        for y in range(4):
            for z in range(4):
                for x in range(2):
                    for c in range(2):
                        there = move(p, y, z, x, c)
                        if there is None:
                            continue
                        q, v, w, u, d = there
                        source = ((p * 4 + y) * 4 + z) * 4 + x * 2 + c
                        target = ((q * 4 + v % 4) * 4 + w % 4) * 4 + u * 2 + d
                        found.append((source, target))
    return found


CORE = pairs(lambda p, y, z, x, c: (p, y, z, x, 1 - c))
CHIP = pairs(lambda p, y, z, x, c: (p, y, z, 1 - x, c))
ONWARD = pairs(lambda p, y, z, x, c: (1, y, z, 1 - x, c) if p == 0 else None)
BACK = pairs(lambda p, y, z, x, c: (0, y, z, 1 - x, c) if p == 1 else None)
Y_UP = pairs(lambda p, y, z, x, c: (p, y + 1, z, x, c))
Y_DOWN = pairs(lambda p, y, z, x, c: (p, y - 1, z, x, c))
Z_UP = pairs(lambda p, y, z, x, c: (p, y, z + 1, x, c))
Z_DOWN = pairs(lambda p, y, z, x, c: (p, y, z - 1, x, c))
Y_ONE = pairs(lambda p, y, z, x, c: (p, y ^ 1, z, x, c))
Y_TWO = pairs(lambda p, y, z, x, c: (p, y ^ 2, z, x, c))
Z_ONE = pairs(lambda p, y, z, x, c: (p, y, z ^ 1, x, c))
Z_TWO = pairs(lambda p, y, z, x, c: (p, y, z ^ 2, x, c))


def send(value, moves):
    return lax.ppermute(value, AXES, moves)


def rows(value, start, size):
    return lax.dynamic_slice_in_dim(value, start, size, 0)


def part(value, index):
    return lax.dynamic_index_in_dim(value, index % 4, 0, keepdims=False)


def dot(left, right):
    return jnp.dot(left, right, preferred_element_type=jnp.float32)


def dot_t(left, right):
    return lax.dot_general(
        left, right, (((1,), (1,)), ((), ())), preferred_element_type=jnp.float32
    )


def t_dot(left, right):
    return lax.dot_general(
        left, right, (((0,), (0,)), ((), ())), preferred_element_type=jnp.float32
    )


def low(value):
    return value.astype(jnp.bfloat16)


def wide(value):
    return value.astype(jnp.float32)


def standardize(values):
    centered = values - jnp.mean(values, -1, keepdims=True)
    variance = jnp.mean(centered * centered, -1, keepdims=True)
    inverse = lax.rsqrt(variance + 1e-05)
    return centered * inverse, inverse


def standardize_back(grad, hat, inverse):
    return inverse * (
        grad
        - jnp.mean(grad, -1, keepdims=True)
        - hat * jnp.mean(grad * hat, -1, keepdims=True)
    )


def in_order(first, second, swap):
    return jnp.where(
        swap, jnp.concatenate([second, first], 0), jnp.concatenate([first, second], 0)
    )


def chip_sum(value, core):
    half = value.shape[0] // 2
    return rows(value, core * half, half) + send(rows(value, (1 - core) * half, half), CORE)


def whole_rows(half, core):
    return in_order(half, send(half, CORE), core == 1)


def tensor_sum(value, core):
    half = chip_sum(value, core)
    return whole_rows(half + send(half, CHIP), core)


def quarter_sum(value, core, place):
    half = chip_sum(value, core)
    size = half.shape[0] // 2
    return rows(half, place * size, size) + send(rows(half, (1 - place) * size, size), CHIP)


def scatter_ring(value, me, up, down):
    far = part(value, me + 2)
    cut = far.shape[0] // 2
    from_down, from_up = send(far[:cut], up), send(far[cut:], down)
    above, below = part(value, me + 1), part(value, me + 3)
    above = jnp.concatenate([above[:cut] + from_down, above[cut:]], 0)
    below = jnp.concatenate([below[:cut], below[cut:] + from_up], 0)
    return part(value, me) + send(above, up) + send(below, down)


def gather_ring(value, up, down):
    below, above = send(value, up), send(value, down)
    cut = value.shape[0] // 2
    far = jnp.concatenate([send(below[:cut], up), send(above[cut:], down)], 0)
    return jnp.stack([value, above, far, below])


def ring_sum(value, first, second):
    shape = value.shape
    here, up, down = first
    there, up2, down2 = second
    total = value.reshape(4, 4, shape[0] // 16, shape[1])
    total = scatter_ring(total, here, up, down)
    total = scatter_ring(total, there, up2, down2)
    total = gather_ring(total, up2, down2)
    total = gather_ring(total, up, down)
    return jnp.roll(total, (here, there), (0, 1)).reshape(shape)


def body(
    inputs,
    memories,
    compressed,
    documents,
    cotangent,
    compressed_cotangent,
    query_weight,
    key_weight,
    value_weight,
    output_weight,
    output_bias,
    inner_weight,
    inner_bias,
    outer_weight,
    outer_bias,
    conv_weight,
    conv_bias,
    attn_gain,
    attn_shift,
    ffn_gain,
    ffn_shift,
):
    section = lax.axis_index("pipe")
    group = lax.axis_index("dp")
    member = lax.axis_index("tensor")
    core, chip = member % 2, member // 2
    y_axis = (group // 4, Y_UP, Y_DOWN)
    z_axis = (group % 4, Z_UP, Z_DOWN)
    context = documents.shape[1]
    width = inputs.shape[1]
    local = query_weight.shape[2]
    heads = local // HEAD_DIM
    held = context - SEG
    quarter = SEG // 4
    scale = HEAD_DIM ** (-0.5)
    query_w, key_w, value_w, output_w = (
        query_weight[0],
        key_weight[0],
        value_weight[0],
        output_weight[0],
    )
    inner_w, outer_w = inner_weight[0], outer_weight[0]
    output_b, inner_b, outer_b = wide(output_bias[0]), wide(inner_bias[0]), wide(outer_bias[0])
    gain_a, shift_a = wide(attn_gain[0]), wide(attn_shift[0])
    gain_f, shift_f = wide(ffn_gain[0]), wide(ffn_shift[0])
    first = section == 0

    memory, older = memories[0, 0], compressed[0, 0]
    squeeze_rows = memory.reshape(COMP, RATE * width)
    squeeze_cot = compressed_cotangent[0, 0]
    conv_g = t_dot(squeeze_rows, squeeze_cot).reshape(RATE, width, local)
    conv_g = lax.psum(conv_g, "dp")
    conv_bg = jnp.sum(wide(squeeze_cot), 0)
    squeezed = dot(squeeze_rows, conv_weight[0].reshape(RATE * width, local)) + wide(conv_bias[0])
    kept_old = lax.dynamic_slice_in_dim(older[COMP:], member * local, local, 1)
    new_compressed = jnp.concatenate([kept_old, low(squeezed)], 0)

    memory_hat, _ = standardize(wide(jnp.concatenate([older, memory], 0)))
    memory_low = low(memory_hat * gain_a + shift_a)
    memory_keys = low(dot(memory_low, key_w))
    memory_values = low(dot(memory_low, value_w))
    positions = jnp.arange(context, dtype=jnp.int32)
    allowed = (positions[None, :] <= positions[held:, None]) & (
        documents[0, held:, None] == documents[0, None, :]
    )

    def head(value, index):
        return value[:, index * HEAD_DIM : (index + 1) * HEAD_DIM]

    def attend(layer_input):
        hat, inverse = standardize(layer_input)
        normed = low(hat * gain_a + shift_a)
        queries = low(dot(normed, query_w))
        keys = jnp.concatenate([memory_keys, low(dot(normed, key_w))], 0)
        values = jnp.concatenate([memory_values, low(dot(normed, value_w))], 0)
        mixed, probs = [], []
        for index in range(heads):
            scores = dot_t(head(queries, index), head(keys, index)) * scale
            scores = jnp.where(allowed, scores, -1e30)
            exps = jnp.exp(scores - jnp.max(scores, -1, keepdims=True))
            probs.append(exps / jnp.sum(exps, -1, keepdims=True))
            mixed.append(low(dot(low(probs[-1]), head(values, index))))
        mixed = jnp.concatenate(mixed, 1)
        attended = tensor_sum(dot(mixed, output_w), core) + output_b
        hidden = layer_input + attended
        return hidden, (hat, inverse, normed, queries, keys, values, probs, mixed)

    def feed(hidden):
        hat, inverse = standardize(hidden)
        normed = low(hat * gain_f + shift_f)
        pre = dot(normed, inner_w) + inner_b
        acts = low(jax.nn.gelu(pre))
        return dot(acts, outer_w), (hat, inverse, normed, pre, acts)

    def feed_back(grad_out, kept):
        hat, inverse, normed, pre, acts = kept
        branch_grad = low(grad_out)
        unused, pull = jax.vjp(jax.nn.gelu, pre)
        pre_grad = low(pull(dot_t(branch_grad, outer_w))[0])
        normed_part = dot_t(pre_grad, inner_w)
        normed_grad = tensor_sum(normed_part, core)
        hidden_grad = grad_out + standardize_back(normed_grad * gain_f, hat, inverse)
        return hidden_grad, (branch_grad, pre_grad, normed_part)

    def attend_back(hidden_grad, kept):
        hat, inverse, normed, queries, keys, values, probs, mixed = kept
        attend_grad = low(hidden_grad)
        mixed_grad = low(dot_t(attend_grad, output_w))
        query_rows, key_rows, value_rows = [], [], []
        for index in range(heads):
            probs_grad = dot_t(head(mixed_grad, index), head(values, index))
            inner = jnp.sum(probs[index] * probs_grad, -1, keepdims=True)
            score_grad = low(probs[index] * (probs_grad - inner))
            query_rows.append(low(dot(score_grad, head(keys, index)) * scale))
            key_rows.append(low(t_dot(score_grad, head(queries, index)) * scale))
            value_rows.append(low(t_dot(low(probs[index]), head(mixed_grad, index))))
        query_rows = jnp.concatenate(query_rows, 1)
        key_rows = jnp.concatenate(key_rows, 1)
        value_rows = jnp.concatenate(value_rows, 1)
        normed_part = (
            dot_t(query_rows, query_w)
            + dot_t(key_rows[held:], key_w)
            + dot_t(value_rows[held:], value_w)
        )
        return normed_part, (attend_grad, query_rows, key_rows, value_rows)

    def pass_on(total, moves, receives, place):
        piece = jnp.where(receives, send(total, moves), total)
        half = in_order(piece, send(piece, CHIP), place == 1)
        return whole_rows(half, core)

    seg_inputs, seg_cot = wide(inputs), wide(cotangent)

    place = jnp.where(first, chip, 1 - chip)
    hidden, kept_a = attend(seg_inputs)
    branch, kept_f = feed(hidden)
    total = quarter_sum(branch, core, place) + outer_b
    total = total + rows(hidden, core * 2 * quarter + place * quarter, quarter)
    forward = pass_on(total, ONWARD, section == 1, place)

    layer_input = jnp.where(first, seg_inputs, forward)
    hidden, kept_a = attend(layer_input)
    branch, kept_f = feed(hidden)
    last_out = hidden + tensor_sum(branch, core) + outer_b
    layer_out = jnp.where(first, forward, last_out)

    hat_a, inverse_a = kept_a[0], kept_a[1]
    place = jnp.where(first, 1 - chip, chip)
    hidden_grad, kept_b = feed_back(seg_cot, kept_f)
    normed_part, kept_c = attend_back(hidden_grad, kept_a)
    total = quarter_sum(normed_part, core, place) * gain_a
    spot = core * 2 * quarter + place * quarter
    total = standardize_back(total, rows(hat_a, spot, quarter), rows(inverse_a, spot, quarter))
    total = total + rows(hidden_grad, spot, quarter)
    backward = pass_on(total, BACK, first, place)

    grad_out = jnp.where(first, backward, seg_cot)
    hidden_grad, (branch_grad, pre_grad, normed_f_part) = feed_back(grad_out, kept_f)
    hat_f, inverse_f, normed_f, pre, acts = kept_f
    outer_g = t_dot(acts, branch_grad)
    inner_g = t_dot(normed_f, pre_grad)
    normed_part, kept_c = attend_back(hidden_grad, kept_a)
    attend_grad, query_rows, key_rows, value_rows = kept_c
    total = hidden_grad + standardize_back(tensor_sum(normed_part, core) * gain_a, hat_a, inverse_a)
    input_grads = jnp.where(first, total, backward)

    normed, mixed = kept_a[2], kept_a[7]
    all_normed = jnp.concatenate([memory_low, normed], 0)
    query_g = t_dot(normed, query_rows)
    key_g = t_dot(all_normed, key_rows)
    value_g = t_dot(all_normed, value_rows)
    output_g = t_dot(mixed, attend_grad)
    memory_part = dot_t(key_rows[:held], key_w) + dot_t(value_rows[:held], value_w)

    small = jnp.stack(
        [
            jnp.sum(memory_part * memory_hat, 0) + jnp.sum(normed_part * hat_a, 0),
            jnp.sum(memory_part, 0) + jnp.sum(normed_part, 0),
            jnp.sum(normed_f_part * hat_f, 0),
            jnp.sum(normed_f_part, 0),
        ]
    )
    small = small + send(small, CORE)
    small = small + send(small, CHIP)
    own = jnp.stack(
        [
            jnp.sum(wide(attend_grad), 0),
            jnp.sum(wide(branch_grad), 0),
            jnp.sum(wide(pre_grad), 0),
            jnp.pad(conv_bg, (0, width - local)),
        ]
    )
    small = jnp.concatenate([small, own], 0)
    for moves in (Y_ONE, Y_TWO, Z_ONE, Z_TWO):
        small = small + send(small, moves)

    outer_g = ring_sum(outer_g, y_axis, z_axis)
    inner_g = ring_sum(inner_g, z_axis, y_axis)
    left = jnp.concatenate([query_g, key_g], 1)
    left = ring_sum(left, y_axis, z_axis)
    query_g, key_g = left[:, :local], left[:, local:]
    right = jnp.concatenate([value_g.reshape(local, width), output_g], 0)
    right = ring_sum(right, z_axis, y_axis)
    value_g, output_g = right[:local].reshape(width, local), right[local:]
    return (
        layer_out[None],
        new_compressed[None, None],
        input_grads[None],
        query_g[None],
        key_g[None],
        value_g[None],
        output_g[None],
        small[4][None],
        inner_g[None],
        small[6][None],
        outer_g[None],
        small[5][None],
        conv_g[None],
        small[7, :local][None],
        small[0][None],
        small[1][None],
        small[2][None],
        small[3][None],
    )


def solution(mesh):
    return jax.shard_map(
        body,
        mesh=mesh,
        in_specs=(
            P("dp", None),
            P("pipe", "dp", None, None),
            P("pipe", "dp", None, None),
            P("dp", None),
            P("dp", None),
            P("pipe", "dp", None, "tensor"),
            P("pipe", None, "tensor"),
            P("pipe", None, "tensor"),
            P("pipe", None, "tensor"),
            P("pipe", "tensor", None),
            P("pipe", None),
            P("pipe", None, "tensor"),
            P("pipe", "tensor"),
            P("pipe", "tensor", None),
            P("pipe", None),
            P("pipe", None, None, "tensor"),
            P("pipe", "tensor"),
            P("pipe", None),
            P("pipe", None),
            P("pipe", None),
            P("pipe", None),
        ),
        out_specs=(
            P("pipe", "dp", None),
            P("pipe", "dp", None, "tensor"),
            P("pipe", "dp", None),
            P("pipe", None, "tensor"),
            P("pipe", None, "tensor"),
            P("pipe", None, "tensor"),
            P("pipe", "tensor", None),
            P("pipe", None),
            P("pipe", None, "tensor"),
            P("pipe", "tensor"),
            P("pipe", "tensor", None),
            P("pipe", None),
            P("pipe", None, None, "tensor"),
            P("pipe", "tensor"),
            P("pipe", None),
            P("pipe", None),
            P("pipe", None),
            P("pipe", None),
        ),
        check_vma=False,
    )
```

time: 1620 us -> 680 us (0.42)
  waiting for transfers between devices: 751 us -> 288 us
  blocking collectives: 354 us -> 0 us
  matrix products: 244 us -> 74 us
  starting transfers between devices: 28.6 us -> 109 us
  other arithmetic: 140 us -> 111 us
    psum x21 -> x1, waiting for transfers between devices: 645 us -> 0.01 us  [body(): conv_g = lax.psum(conv_g, 'dp')]
    psum x2 -> x0, blocking collectives: 354 us -> none  [the longest x1 278 us: body(): lax.psum((gain_ag, shift_ag, gain_fg, shift_fg), ('dp', 'tensor'))]
    ppermute x8 -> x98, waiting for transfers between devices: 106 us -> 288 us  [send(): return lax.ppermute(value, AXES, moves)]
    dot_general x148 -> x58, matrix products: 244 us -> 74 us  [the longest x21 33.5 us: dot_t(): lax.dot_general(left, right, (((1,), (1,)), ((), ())), preferred_element_...]
    ppermute x8 -> x98, starting transfers between devices: 26.3 us -> 109 us  [send(): return lax.ppermute(value, AXES, moves)]
    dynamic_update_slice x19 -> x0, other arithmetic: 29.6 us -> none  [guarded_update(): lax.dynamic_update_slice_in_dim(buffer, jnp.where(valid, piece, current),...]
    reduce_sum x23 -> x5, other arithmetic: 30.2 us -> 5.67 us  [standardize(): centered = values - jnp.mean(values, -1, keepdims=True)]
    unnamed x595 -> x301, local copies, waits for them, and re-layouts: 54.1 us -> 29.6 us
  transfers between devices with their start and end apart: 29 -> 99, of which waited for: 27 -> 44; matrix products, arithmetic and copies ran while one was open for 8% -> 19% of each run, Pallas kernels for 0% -> 0%
where the time goes in v1:
time: 680 us; the launch traced here: 670 us
  waiting for transfers between devices  288 us (42%)
  other arithmetic  111 us (16%)
  starting transfers between devices  109 us (16%)
  matrix products  74 us (11%)
  local copies, waits for them, and re-layouts  70.5 us (10%)
  between operations  17.4 us (3%)
    ppermute x98, waiting for transfers between devices, send(): return lax.ppermute(value, AXES, moves)  288 us
    ppermute x98, starting transfers between devices, send(): return lax.ppermute(value, AXES, moves)  109 us
    dot_general x21, matrix products, dot_t(): lax.dot_general(left, right, (((1,), (1,)), ((), ())), preferred_element_...  33.5 us
    unnamed x301, local copies, waits for them, and re-layouts  29.6 us
    dot_general x22, matrix products, dot(): return jnp.dot(left, right, preferred_element_type=jnp.float32)  24.7 us
    dot_general x15, matrix products, t_dot(): lax.dot_general(left, right, (((0,), (0,)), ((), ())), preferred_element_...  15.8 us
    concatenate x6, other arithmetic, ring_sum(): return jnp.roll(total, (here, there), (0, 1)).reshape(shape)  15.4 us
  transfers between devices with their start and end apart: 99, of which 44 were waited for; matrix products, arithmetic and copies ran while one was open for 19% of the time, Pallas kernels for 0%

profile of v1, /device:TPU:0, one launch (start us, length us, event | category | flops | bytes accessed | tf_op | source)
XLA Modules:
  0.0 669.9 jit_solution(4075425804091166834)
XLA Ops:
  42.8 23.6 %collective-permute-done.1 = f32[256,1024]{1,0:T(8,128)S(1)} collective-permute-done((f32[256,1024]{1,0:T(8,128)S(1)}, f32[256,1024]{1,0:T(8,128)S(1)}, u32[]{:S(2)}, u32[]{:S(2)}) %collective-permute-start.1) | collective-permute-done | bytes 1048608 | tf_op jit(solution)/shard_map/ppermute | solution.py:45
  75.1 6.1 fusion.75
  91.6 12.7 %collective-permute-done.4 = f32[128,1024]{1,0:T(8,128)} collective-permute-done((f32[128,1024]{1,0:T(8,128)}, f32[128,1024]{1,0:T(8,128)}, u32[]{:S(2)}, u32[]{:S(2)}) %collective-permute-start.4) | collective-permute-done | bytes 524320 | tf_op jit(solution)/shard_map/ppermute | solution.py:45
  106.6 5.5 collective-permute-start.5
  112.1 10.2 %collective-permute-done.5 = f32[128,1024]{1,0:T(8,128)} collective-permute-done((f32[128,1024]{1,0:T(8,128)}, f32[128,1024]{1,0:T(8,128)}, u32[]{:S(2)}, u32[]{:S(2)}) %collective-permute-start.5) | collective-permute-done | bytes 524320 | tf_op jit(solution)/shard_map/ppermute | solution.py:45
  124.4 12.3 %collective-permute-done.6 = f32[128,1024]{1,0:T(8,128)} collective-permute-done((f32[128,1024]{1,0:T(8,128)}, f32[128,1024]{1,0:T(8,128)}, u32[]{:S(2)}, u32[]{:S(2)}) %collective-permute-start.6) | collective-permute-done | bytes 524320 | tf_op jit(solution)/shard_map/ppermute | solution.py:45
  158.3 24.9 %collective-permute-done.9 = f32[256,1024]{1,0:T(8,128)S(1)} collective-permute-done((f32[256,1024]{1,0:T(8,128)S(1)}, f32[256,1024]{1,0:T(8,128)S(1)}, u32[]{:S(2)}, u32[]{:S(2)}) %collective-permute-start.9) | collective-permute-done | bytes 1048608 | tf_op jit(solution)/shard_map/ppermute | solution.py:45
  195.2 6.5 fusion.79
  207.5 23.7 %collective-permute-done.12 = f32[256,1024]{1,0:T(8,128)S(1)} collective-permute-done((f32[256,1024]{1,0:T(8,128)S(1)}, f32[256,1024]{1,0:T(8,128)S(1)}, u32[]{:S(2)}, u32[]{:S(2)}) %collective-permute-start.12) | collective-permute-done | bytes 1048608 | tf_op jit(solution)/shard_map/ppermute | solution.py:45
  231.5 21.4 %collective-permute-done.15 = f32[256,1024]{1,0:T(8,128)S(1)} collective-permute-done((f32[256,1024]{1,0:T(8,128)S(1)}, f32[256,1024]{1,0:T(8,128)S(1)}, u32[]{:S(2)}, u32[]{:S(2)}) %collective-permute-start.15) | collective-permute-done | bytes 1048608 | tf_op jit(solution)/shard_map/ppermute | solution.py:45
  256.2 3.8 fusion.217
  285.8 13.3 %collective-permute-done.18 = f32[128,1024]{1,0:T(8,128)} collective-permute-done((f32[128,1024]{1,0:T(8,128)}, f32[128,1024]{1,0:T(8,128)}, u32[]{:S(2)}, u32[]{:S(2)}) %collective-permute-start.18) | collective-permute-done | bytes 524320 | tf_op jit(solution)/shard_map/ppermute | solution.py:45
  303.4 15.0 %collective-permute-done.19 = f32[128,1024]{1,0:T(8,128)S(1)} collective-permute-done((f32[128,1024]{1,0:T(8,128)S(1)}, f32[128,1024]{1,0:T(8,128)S(1)}, u32[]{:S(2)}, u32[]{:S(2)}) %collective-permute-start.19) | collective-permute-done | bytes 524320 | tf_op jit(solution)/shard_map/ppermute | solution.py:45
  319.3 12.6 %collective-permute-done.20 = f32[128,1024]{1,0:T(8,128)} collective-permute-done((f32[128,1024]{1,0:T(8,128)}, f32[128,1024]{1,0:T(8,128)}, u32[]{:S(2)}, u32[]{:S(2)}) %collective-permute-start.20) | collective-permute-done | bytes 524320 | tf_op jit(solution)/shard_map/ppermute | solution.py:45
  337.8 3.7 convert_reduce_fusion.3
  341.5 3.1 convert_reduce_fusion.2
  358.7 7.2 %collective-permute-done.66 = f32[2,64,1024]{2,1,0:T(8,128)S(1)} collective-permute-done((f32[2,64,1024]{2,1,0:T(8,128)S(1)}, f32[2,64,1024]{2,1,0:T(8,128)S(1)}, u32[]{:S(2)}, u32[]{:S(2)}) %collective-permute-start.66) | collective-permute-done | bytes 524320 | tf_op jit(solution)/shard_map/ppermute | solution.py:45
  367.1 3.0 collective-permute-start.69
  386.9 7.8 %collective-permute-done.69 = f32[4,64,1024]{2,1,0:T(8,128)} collective-permute-done((f32[4,64,1024]{2,1,0:T(8,128)}, f32[4,64,1024]{2,1,0:T(8,128)}, u32[]{:S(2)}, u32[]{:S(2)}) %collective-permute-start.69) | collective-permute-done | bytes 1048608 | tf_op jit(solution)/shard_map/ppermute | solution.py:45
  394.8 5.1 collective-permute-done.67
  406.3 5.8 collective-permute-done.83
  414.5 3.2 collective-permute-start.88
  421.6 3.5 collective-permute-start.89
  430.0 3.2 collective-permute-start.74
  435.1 3.2 collective-permute-start.90
  443.4 3.2 collective-permute-start.77
  452.4 3.3 collective-permute-start.93
  464.6 3.9 multiply_reduce_fusion.4
  468.6 4.8 convert_reduce_fusion.4
  500.3 3.3 collective-permute-start.46
  503.6 3.3 fusion.6
  515.0 3.2 collective-permute-done.28
  528.3 17.4 %collective-permute-done.95 = f32[4,64,1024]{2,1,0:T(8,128)S(1)} collective-permute-done((f32[4,64,1024]{2,1,0:T(8,128)}, f32[4,64,1024]{2,1,0:T(8,128)S(1)}, u32[]{:S(2)}, u32[]{:S(2)}) %collective-permute-start.95) | collective-permute-done | bytes 1048608 | tf_op jit(solution)/shard_map/ppermute | solution.py:45
  546.1 6.4 collective-permute-done.29
  556.0 4.2 collective-permute-done.81
  563.5 4.5 fusion.20
  568.2 3.4 collective-permute-start.34
  571.7 3.8 fusion.12
  575.5 3.0 fusion.16
  588.7 3.2 collective-permute-start.36
  598.5 3.3 collective-permute-start.39
  607.2 6.7 %collective-permute-done.56 = f32[4,32,1024]{2,1,0:T(8,128)S(1)} collective-permute-done((f32[4,32,1024]{2,1,0:T(8,128)S(1)}, f32[4,32,1024]{2,1,0:T(8,128)S(1)}, u32[]{:S(2)}, u32[]{:S(2)}) %collective-permute-start.56) | collective-permute-done | bytes 524320 | tf_op jit(solution)/shard_map/ppermute | solution.py:45
  619.4 3.9 collective-permute-done.43
  633.2 3.2 collective-permute-done.61
  642.6 3.8 collective-permute-done.63
  646.4 3.9 collective-permute-done.64
  653.2 5.0 select_bitcast_fusion
  659.4 3.2 copy.64
  (710 shorter events, 307.9 us)
Async XLA Ops:
  7.2 652.2 %all-reduce.3.cloned.1.call-start = ((), (), s32[]{:S(2)}) async-start(), calls=%async_computation | async-start | bytes 4194304 | tf_op jit(solution)/shard_map/psum | solution.py:202
  41.2 25.3 %collective-permute-start.1 = (f32[256,1024]{1,0:T(8,128)S(1)}, f32[256,1024]{1,0:T(8,128)S(1)}, u32[]{:S(2)}, u32[]{:S(2)}) collective-permute-start(f32[256,1024]{1,0:T(8,128)S(1)} %dynamic-slice_add_fusion.7), channel_id=1, source_target_pairs={{0,2},{1,3},{2,0},{3,1},{4,6},{5,7},{6,4},{7,5},{8,10},{9,11},{10,... | collective-permute-start | bytes 3145736 | tf_op jit(solution)/shard_map/ppermute | solution.py:45
  90.0 14.3 %collective-permute-start.4 = (f32[128,1024]{1,0:T(8,128)}, f32[128,1024]{1,0:T(8,128)}, u32[]{:S(2)}, u32[]{:S(2)}) collective-permute-start(f32[128,1024]{1,0:T(8,128)} %constant_dynamic-slice_fusion.9), channel_id=1, source_target_pairs={{0,2},{1,3},{2,0},{3,1},{4,6},{5,7},{6,4},{7,5},{8,10},{9,11},{10,... | collective-permute-start | bytes 1572872 | tf_op jit(solution)/shard_map/ppermute | solution.py:45
  106.6 15.7 %collective-permute-start.5 = (f32[128,1024]{1,0:T(8,128)}, f32[128,1024]{1,0:T(8,128)}, u32[]{:S(2)}, u32[]{:S(2)}) collective-permute-start(f32[128,1024]{1,0:T(8,128)} %dynamic-slice_add_fusion.9), channel_id=1, source_target_pairs={{0,66},{1,67},{2,64},{3,65},{4,70},{5,71},{6,68},{7,69},{8,74},{9,... | collective-permute-start | bytes 1572872 | tf_op jit(solution)/shard_map/ppermute | solution.py:45
  124.2 12.5 %collective-permute-start.6 = (f32[128,1024]{1,0:T(8,128)}, f32[128,1024]{1,0:T(8,128)}, u32[]{:S(2)}, u32[]{:S(2)}) collective-permute-start(f32[128,1024]{1,0:T(8,128)} %broadcast_select_fusion.1), channel_id=1, source_target_pairs={{0,2},{1,3},{2,0},{3,1},{4,6},{5,7},{6,4},{7,5},{8,10},{9,11},{10,... | collective-permute-start | bytes 1572872 | tf_op jit(solution)/shard_map/ppermute | solution.py:45
  158.0 25.3 %collective-permute-start.9 = (f32[256,1024]{1,0:T(8,128)S(1)}, f32[256,1024]{1,0:T(8,128)S(1)}, u32[]{:S(2)}, u32[]{:S(2)}) collective-permute-start(f32[256,1024]{1,0:T(8,128)S(1)} %dynamic-slice_add_fusion.5), channel_id=1, source_target_pairs={{0,2},{1,3},{2,0},{3,1},{4,6},{5,7},{6,4},{7,5},{8,10},{9,11},{10,... | collective-permute-start | bytes 3145736 | tf_op jit(solution)/shard_map/ppermute | solution.py:45
  205.1 26.1 %collective-permute-start.12 = (f32[256,1024]{1,0:T(8,128)S(1)}, f32[256,1024]{1,0:T(8,128)S(1)}, u32[]{:S(2)}, u32[]{:S(2)}) collective-permute-start(f32[256,1024]{1,0:T(8,128)S(1)} %dynamic-slice_add_fusion.4), channel_id=1, source_target_pairs={{0,2},{1,3},{2,0},{3,1},{4,6},{5,7},{6,4},{7,5},{8,10},{9,11},{10,... | collective-permute-start | bytes 3145736 | tf_op jit(solution)/shard_map/ppermute | solution.py:45
  206.0 46.9 %collective-permute-start.15 = (f32[256,1024]{1,0:T(8,128)S(1)}, f32[256,1024]{1,0:T(8,128)S(1)}, u32[]{:S(2)}, u32[]{:S(2)}) collective-permute-start(f32[256,1024]{1,0:T(8,128)S(1)} %dynamic-slice_add_fusion.3), channel_id=1, source_target_pairs={{0,2},{1,3},{2,0},{3,1},{4,6},{5,7},{6,4},{7,5},{8,10},{9,11},{10,... | collective-permute-start | bytes 3145736 | tf_op jit(solution)/shard_map/ppermute | solution.py:45
  231.4 22.2 %collective-permute-start.13 = (f32[256,1024]{1,0:T(8,128)S(1)}, f32[256,1024]{1,0:T(8,128)S(1)}, u32[]{:S(2)}, u32[]{:S(2)}) collective-permute-start(f32[256,1024]{1,0:T(8,128)S(1)} %add.701), channel_id=1, source_target_pairs={{0,1},{1,0},{2,3},{3,2},{4,5},{5,4},{6,7},{7,6},{8,9},{9,8},{10,11... | collective-permute-start | bytes 3145736 | tf_op jit(solution)/shard_map/ppermute | solution.py:45
  284.8 14.3 %collective-permute-start.18 = (f32[128,1024]{1,0:T(8,128)}, f32[128,1024]{1,0:T(8,128)}, u32[]{:S(2)}, u32[]{:S(2)}) collective-permute-start(f32[128,1024]{1,0:T(8,128)} %constant_dynamic-slice_fusion.4), channel_id=1, source_target_pairs={{0,2},{1,3},{2,0},{3,1},{4,6},{5,7},{6,4},{7,5},{8,10},{9,11},{10,... | collective-permute-start | bytes 1572872 | tf_op jit(solution)/shard_map/ppermute | solution.py:45
  302.1 16.3 %collective-permute-start.19 = (f32[128,1024]{1,0:T(8,128)S(1)}, f32[128,1024]{1,0:T(8,128)S(1)}, u32[]{:S(2)}, u32[]{:S(2)}) collective-permute-start(f32[128,1024]{1,0:T(8,128)S(1)} %dynamic-slice_add_fusion.8), channel_id=1, source_target_pairs={{64,2},{65,3},{66,0},{67,1},{68,6},{69,7},{70,4},{71,5},{72,10},{7... | collective-permute-start | bytes 1572872 | tf_op jit(solution)/shard_map/ppermute | solution.py:45
  319.3 12.6 %collective-permute-start.20 = (f32[128,1024]{1,0:T(8,128)}, f32[128,1024]{1,0:T(8,128)}, u32[]{:S(2)}, u32[]{:S(2)}) collective-permute-start(f32[128,1024]{1,0:T(8,128)} %broadcast_select_fusion), channel_id=1, source_target_pairs={{0,2},{1,3},{2,0},{3,1},{4,6},{5,7},{6,4},{7,5},{8,10},{9,11},{10,... | collective-permute-start | bytes 1572872 | tf_op jit(solution)/shard_map/ppermute | solution.py:45
  348.9 36.0 %collective-permute-start.22 = (f32[256,1024]{1,0:T(8,128)}, f32[256,1024]{1,0:T(8,128)}, u32[]{:S(2)}, u32[]{:S(2)}) collective-permute-start(f32[256,1024]{1,0:T(8,128)} %constant_dynamic-slice_fusion.3), channel_id=1, source_target_pairs={{0,1},{1,0},{2,3},{3,2},{4,5},{5,4},{6,7},{7,6},{8,9},{9,8},{10,11... | collective-permute-start | bytes 3145736 | tf_op jit(solution)/shard_map/ppermute | solution.py:45
  349.3 16.6 %collective-permute-start.66 = (f32[2,64,1024]{2,1,0:T(8,128)S(1)}, f32[2,64,1024]{2,1,0:T(8,128)S(1)}, u32[]{:S(2)}, u32[]{:S(2)}) collective-permute-start(f32[2,64,1024]{2,1,0:T(8,128)S(1)} %get-tuple-element.52), channel_id=1, source_target_pairs={{0,4},{1,5},{2,6},{3,7},{4,8},{5,9},{6,10},{7,11},{8,12},{9,13},{1... | collective-permute-start | bytes 1572872 | tf_op jit(solution)/shard_map/ppermute | solution.py:45
  351.3 14.6 %collective-permute-start.68 = (f32[2,64,1024]{2,1,0:T(8,128)S(1)}, f32[2,64,1024]{2,1,0:T(8,128)S(1)}, u32[]{:S(2)}, u32[]{:S(2)}) collective-permute-start(f32[2,64,1024]{2,1,0:T(8,128)S(1)} %get-tuple-element.54), channel_id=1, source_target_pairs={{0,12},{1,13},{2,14},{3,15},{4,0},{5,1},{6,2},{7,3},{8,4},{9,5},{1... | collective-permute-start | bytes 1572872 | tf_op jit(solution)/shard_map/ppermute | solution.py:45
  355.4 15.8 %collective-permute-start.82 = (f32[2,64,1024]{2,1,0:T(8,128)S(1)}, f32[2,64,1024]{2,1,0:T(8,128)S(1)}, u32[]{:S(2)}, u32[]{:S(2)}) collective-permute-start(f32[2,64,1024]{2,1,0:T(8,128)S(1)} %get-tuple-element.46), channel_id=1, source_target_pairs={{0,16},{1,17},{2,18},{3,19},{4,20},{5,21},{6,22},{7,23},{8,24},{9,... | collective-permute-start | bytes 1572872 | tf_op jit(solution)/shard_map/ppermute | solution.py:45
  357.0 14.2 %collective-permute-start.84 = (f32[2,64,1024]{2,1,0:T(8,128)S(1)}, f32[2,64,1024]{2,1,0:T(8,128)S(1)}, u32[]{:S(2)}, u32[]{:S(2)}) collective-permute-start(f32[2,64,1024]{2,1,0:T(8,128)S(1)} %get-tuple-element.48), channel_id=1, source_target_pairs={{0,48},{1,49},{2,50},{3,51},{4,52},{5,53},{6,54},{7,55},{8,56},{9,... | collective-permute-start | bytes 1572872 | tf_op jit(solution)/shard_map/ppermute | solution.py:45
  367.1 27.7 %collective-permute-start.69 = (f32[4,64,1024]{2,1,0:T(8,128)}, f32[4,64,1024]{2,1,0:T(8,128)}, u32[]{:S(2)}, u32[]{:S(2)}) collective-permute-start(f32[4,64,1024]{2,1,0:T(8,128)} %pad_maximum_fusion.7), channel_id=1, source_target_pairs={{0,12},{1,13},{2,14},{3,15},{4,0},{5,1},{6,2},{7,3},{8,4},{9,5},{1... | collective-permute-start | bytes 3145736 | tf_op jit(solution)/shard_map/ppermute | solution.py:45
  371.2 28.7 %collective-permute-start.67 = (f32[4,64,1024]{2,1,0:T(8,128)}, f32[4,64,1024]{2,1,0:T(8,128)}, u32[]{:S(2)}, u32[]{:S(2)}) collective-permute-start(f32[4,64,1024]{2,1,0:T(8,128)} %pad_maximum_fusion.6), channel_id=1, source_target_pairs={{0,4},{1,5},{2,6},{3,7},{4,8},{5,9},{6,10},{7,11},{8,12},{9,13},{1... | collective-permute-start | bytes 3145736 | tf_op jit(solution)/shard_map/ppermute | solution.py:45
  372.5 33.9 %collective-permute-start.85 = (f32[4,64,1024]{2,1,0:T(8,128)}, f32[4,64,1024]{2,1,0:T(8,128)}, u32[]{:S(2)}, u32[]{:S(2)}) collective-permute-start(f32[4,64,1024]{2,1,0:T(8,128)} %pad_maximum_fusion.10), channel_id=1, source_target_pairs={{0,48},{1,49},{2,50},{3,51},{4,52},{5,53},{6,54},{7,55},{8,56},{9,... | collective-permute-start | bytes 3145736 | tf_op jit(solution)/shard_map/ppermute | solution.py:45
  376.6 35.6 %collective-permute-start.83 = (f32[4,64,1024]{2,1,0:T(8,128)}, f32[4,64,1024]{2,1,0:T(8,128)}, u32[]{:S(2)}, u32[]{:S(2)}) collective-permute-start(f32[4,64,1024]{2,1,0:T(8,128)} %pad_maximum_fusion.9), channel_id=1, source_target_pairs={{0,16},{1,17},{2,18},{3,19},{4,20},{5,21},{6,22},{7,23},{8,24},{9,... | collective-permute-start | bytes 3145736 | tf_op jit(solution)/shard_map/ppermute | solution.py:45
  386.6 46.7 %collective-permute-start.23 = (f32[256,1024]{1,0:T(8,128)S(1)}, f32[256,1024]{1,0:T(8,128)S(1)}, u32[]{:S(2)}, u32[]{:S(2)}) collective-permute-start(f32[256,1024]{1,0:T(8,128)S(1)} %dynamic-slice_add_fusion.1), channel_id=1, source_target_pairs={{0,2},{1,3},{2,0},{3,1},{4,6},{5,7},{6,4},{7,5},{8,10},{9,11},{10,... | collective-permute-start | bytes 3145736 | tf_op jit(solution)/shard_map/ppermute | solution.py:45
  402.1 15.6 %collective-permute-start.70 = (f32[32,1024]{1,0:T(8,128)S(1)}, f32[32,1024]{1,0:T(8,128)S(1)}, u32[]{:S(2)}, u32[]{:S(2)}) collective-permute-start(f32[32,1024]{1,0:T(8,128)S(1)} %get-tuple-element.85), channel_id=1, source_target_pairs={{0,16},{1,17},{2,18},{3,19},{4,20},{5,21},{6,22},{7,23},{8,24},{9,... | collective-permute-start | bytes 393224 | tf_op jit(solution)/shard_map/ppermute | solution.py:45
  404.3 13.4 %collective-permute-start.72 = (f32[32,1024]{1,0:T(8,128)S(1)}, f32[32,1024]{1,0:T(8,128)S(1)}, u32[]{:S(2)}, u32[]{:S(2)}) collective-permute-start(f32[32,1024]{1,0:T(8,128)S(1)} %get-tuple-element.87), channel_id=1, source_target_pairs={{0,48},{1,49},{2,50},{3,51},{4,52},{5,53},{6,54},{7,55},{8,56},{9,... | collective-permute-start | bytes 393224 | tf_op jit(solution)/shard_map/ppermute | solution.py:45
  421.6 12.7 %collective-permute-start.89 = (f32[64,1024]{1,0:T(8,128)S(1)}, f32[64,1024]{1,0:T(8,128)S(1)}, u32[]{:S(2)}, u32[]{:S(2)}) collective-permute-start(f32[64,1024]{1,0:T(8,128)S(1)} %pad_maximum_fusion.33), channel_id=1, source_target_pairs={{0,12},{1,13},{2,14},{3,15},{4,0},{5,1},{6,2},{7,3},{8,4},{9,5},{1... | collective-permute-start | bytes 786440 | tf_op jit(solution)/shard_map/ppermute | solution.py:45
  434.3 30.3 %collective-permute-start.24 = (f32[256,1024]{1,0:T(8,128)}, f32[256,1024]{1,0:T(8,128)}, u32[]{:S(2)}, u32[]{:S(2)}) collective-permute-start(f32[256,1024]{1,0:T(8,128)} %add.723), channel_id=1, source_target_pairs={{0,1},{1,0},{2,3},{3,2},{4,5},{5,4},{6,7},{7,6},{8,9},{9,8},{10,11... | collective-permute-start | bytes 3145736 | tf_op jit(solution)/shard_map/ppermute | solution.py:45
  435.1 15.4 %collective-permute-start.91 = (f32[64,1024]{1,0:T(8,128)}, f32[64,1024]{1,0:T(8,128)}, u32[]{:S(2)}, u32[]{:S(2)}) collective-permute-start(f32[64,1024]{1,0:T(8,128)} %fusion.190), channel_id=1, source_target_pairs={{0,4},{1,5},{2,6},{3,7},{4,8},{5,9},{6,10},{7,11},{8,12},{9,13},{1... | collective-permute-start | bytes 786440 | tf_op jit(solution)/shard_map/ppermute | solution.py:45
  435.1 16.4 %collective-permute-start.90 = (f32[64,1024]{1,0:T(8,128)}, f32[64,1024]{1,0:T(8,128)}, u32[]{:S(2)}, u32[]{:S(2)}) collective-permute-start(f32[64,1024]{1,0:T(8,128)} %fusion.190), channel_id=1, source_target_pairs={{0,12},{1,13},{2,14},{3,15},{4,0},{5,1},{6,2},{7,3},{8,4},{9,5},{1... | collective-permute-start | bytes 786440 | tf_op jit(solution)/shard_map/ppermute | solution.py:45
  441.8 13.9 %collective-permute-start.76 = (f32[32,1024]{1,0:T(8,128)}, f32[32,1024]{1,0:T(8,128)}, u32[]{:S(2)}, u32[]{:S(2)}) collective-permute-start(f32[32,1024]{1,0:T(8,128)} %slice.644), channel_id=1, source_target_pairs={{0,16},{1,17},{2,18},{3,19},{4,20},{5,21},{6,22},{7,23},{8,24},{9,... | collective-permute-start | bytes 393224 | tf_op jit(solution)/shard_map/ppermute | solution.py:45
  459.4 60.9 %collective-permute-start.78 = (f32[4,64,1024]{2,1,0:T(8,128)}, f32[4,64,1024]{2,1,0:T(8,128)}, u32[]{:S(2)}, u32[]{:S(2)}) collective-permute-start(f32[4,64,1024]{2,1,0:T(8,128)} %get-tuple-element.81), channel_id=1, source_target_pairs={{0,12},{1,13},{2,14},{3,15},{4,0},{5,1},{6,2},{7,3},{8,4},{9,5},{1... | collective-permute-start | bytes 3145736 | tf_op jit(solution)/shard_map/ppermute | solution.py:45
  459.4 63.0 %collective-permute-start.79 = (f32[4,64,1024]{2,1,0:T(8,128)}, f32[4,64,1024]{2,1,0:T(8,128)}, u32[]{:S(2)}, u32[]{:S(2)}) collective-permute-start(f32[4,64,1024]{2,1,0:T(8,128)} %get-tuple-element.81), channel_id=1, source_target_pairs={{0,4},{1,5},{2,6},{3,7},{4,8},{5,9},{6,10},{7,11},{8,12},{9,13},{1... | collective-permute-start | bytes 3145736 | tf_op jit(solution)/shard_map/ppermute | solution.py:45
  464.2 59.7 %collective-permute-start.94 = (f32[4,64,1024]{2,1,0:T(8,128)}, f32[4,64,1024]{2,1,0:T(8,128)}, u32[]{:S(2)}, u32[]{:S(2)}) collective-permute-start(f32[4,64,1024]{2,1,0:T(8,128)} %get-tuple-element.73), channel_id=1, source_target_pairs={{0,48},{1,49},{2,50},{3,51},{4,52},{5,53},{6,54},{7,55},{8,56},{9,... | collective-permute-start | bytes 3145736 | tf_op jit(solution)/shard_map/ppermute | solution.py:45
  518.2 27.5 %collective-permute-start.95 = (f32[4,64,1024]{2,1,0:T(8,128)}, f32[4,64,1024]{2,1,0:T(8,128)S(1)}, u32[]{:S(2)}, u32[]{:S(2)}) collective-permute-start(f32[4,64,1024]{2,1,0:T(8,128)} %get-tuple-element.73), channel_id=1, source_target_pairs={{0,16},{1,17},{2,18},{3,19},{4,20},{5,21},{6,22},{7,23},{8,24},{9,... | collective-permute-start | bytes 3145736 | tf_op jit(solution)/shard_map/ppermute | solution.py:45
  520.0 33.7 %collective-permute-start.47 = (f32[4,32,1024]{2,1,0:T(8,128)S(1)}, f32[4,32,1024]{2,1,0:T(8,128)S(1)}, u32[]{:S(2)}, u32[]{:S(2)}) collective-permute-start(f32[4,32,1024]{2,1,0:T(8,128)S(1)} %pad_maximum_fusion.16), channel_id=1, source_target_pairs={{0,12},{1,13},{2,14},{3,15},{4,0},{5,1},{6,2},{7,3},{8,4},{9,5},{1... | collective-permute-start | bytes 1572872 | tf_op jit(solution)/shard_map/ppermute | solution.py:45
  520.3 33.5 %collective-permute-start.45 = (f32[4,32,1024]{2,1,0:T(8,128)S(1)}, f32[4,32,1024]{2,1,0:T(8,128)S(1)}, u32[]{:S(2)}, u32[]{:S(2)}) collective-permute-start(f32[4,32,1024]{2,1,0:T(8,128)S(1)} %pad_maximum_fusion.15), channel_id=1, source_target_pairs={{0,4},{1,5},{2,6},{3,7},{4,8},{5,9},{6,10},{7,11},{8,12},{9,13},{1... | collective-permute-start | bytes 1572872 | tf_op jit(solution)/shard_map/ppermute | solution.py:45
  522.4 23.4 %collective-permute-start.31 = (f32[4,64,512]{2,1,0:T(8,128)S(1)}, f32[4,64,512]{2,1,0:T(8,128)S(1)}, u32[]{:S(2)}, u32[]{:S(2)}) collective-permute-start(f32[4,64,512]{2,1,0:T(8,128)S(1)} %pad_maximum_fusion.13), channel_id=1, source_target_pairs={{0,48},{1,49},{2,50},{3,51},{4,52},{5,53},{6,54},{7,55},{8,56},{9,... | collective-permute-start | bytes 1572872 | tf_op jit(solution)/shard_map/ppermute | solution.py:45
  523.9 28.6 %collective-permute-start.29 = (f32[4,64,512]{2,1,0:T(8,128)S(1)}, f32[4,64,512]{2,1,0:T(8,128)S(1)}, u32[]{:S(2)}, u32[]{:S(2)}) collective-permute-start(f32[4,64,512]{2,1,0:T(8,128)S(1)} %pad_maximum_fusion.12), channel_id=1, source_target_pairs={{0,16},{1,17},{2,18},{3,19},{4,20},{5,21},{6,22},{7,23},{8,24},{9,... | collective-permute-start | bytes 1572872 | tf_op jit(solution)/shard_map/ppermute | solution.py:45
  545.7 61.2 %collective-permute-start.25 = (f32[256,1024]{1,0:T(8,128)S(1)}, f32[256,1024]{1,0:T(8,128)S(1)}, u32[]{:S(2)}, u32[]{:S(2)}) collective-permute-start(f32[256,1024]{1,0:T(8,128)S(1)} %constant_dynamic-slice_fusion.2), channel_id=1, source_target_pairs={{0,1},{1,0},{2,3},{3,2},{4,5},{5,4},{6,7},{7,6},{8,9},{9,8},{10,11... | collective-permute-start | bytes 3145736 | tf_op jit(solution)/shard_map/ppermute | solution.py:45
  545.8 14.4 %collective-permute-start.81 = (f32[2,64,1024]{2,1,0:T(8,128)S(1)}, f32[2,64,1024]{2,1,0:T(8,128)S(1)}, u32[]{:S(2)}, u32[]{:S(2)}) collective-permute-start(f32[2,64,1024]{2,1,0:T(8,128)S(1)} %slice.647), channel_id=1, source_target_pairs={{0,12},{1,13},{2,14},{3,15},{4,0},{5,1},{6,2},{7,3},{8,4},{9,5},{1... | collective-permute-start | bytes 1572872 | tf_op jit(solution)/shard_map/ppermute | solution.py:45
  553.8 14.3 %collective-permute-start.97 = (f32[2,64,1024]{2,1,0:T(8,128)S(1)}, f32[2,64,1024]{2,1,0:T(8,128)S(1)}, u32[]{:S(2)}, u32[]{:S(2)}) collective-permute-start(f32[2,64,1024]{2,1,0:T(8,128)S(1)} %slice.652), channel_id=1, source_target_pairs={{0,48},{1,49},{2,50},{3,51},{4,52},{5,53},{6,54},{7,55},{8,56},{9,... | collective-permute-start | bytes 1572872 | tf_op jit(solution)/shard_map/ppermute | solution.py:45
  553.9 14.3 %collective-permute-start.96 = (f32[2,64,1024]{2,1,0:T(8,128)S(1)}, f32[2,64,1024]{2,1,0:T(8,128)S(1)}, u32[]{:S(2)}, u32[]{:S(2)}) collective-permute-start(f32[2,64,1024]{2,1,0:T(8,128)S(1)} %slice.651), channel_id=1, source_target_pairs={{0,16},{1,17},{2,18},{3,19},{4,20},{5,21},{6,22},{7,23},{8,24},{9,... | collective-permute-start | bytes 1572872 | tf_op jit(solution)/shard_map/ppermute | solution.py:45
  560.2 18.4 %collective-permute-start.48 = (f32[16,1024]{1,0:T(8,128)S(1)}, f32[16,1024]{1,0:T(8,128)S(1)}, u32[]{:S(2)}, u32[]{:S(2)}) collective-permute-start(f32[16,1024]{1,0:T(8,128)S(1)} %get-tuple-element.91), channel_id=1, source_target_pairs={{0,16},{1,17},{2,18},{3,19},{4,20},{5,21},{6,22},{7,23},{8,24},{9,... | collective-permute-start | bytes 196616 | tf_op jit(solution)/shard_map/ppermute | solution.py:45
  563.2 15.3 %collective-permute-start.50 = (f32[16,1024]{1,0:T(8,128)S(1)}, f32[16,1024]{1,0:T(8,128)S(1)}, u32[]{:S(2)}, u32[]{:S(2)}) collective-permute-start(f32[16,1024]{1,0:T(8,128)S(1)} %get-tuple-element.93), channel_id=1, source_target_pairs={{0,48},{1,49},{2,50},{3,51},{4,52},{5,53},{6,54},{7,55},{8,56},{9,... | collective-permute-start | bytes 196616 | tf_op jit(solution)/shard_map/ppermute | solution.py:45
  568.1 12.7 %collective-permute-start.32 = (f32[32,512]{1,0:T(8,128)S(1)}, f32[32,512]{1,0:T(8,128)S(1)}, u32[]{:S(2)}, u32[]{:S(2)}) collective-permute-start(f32[32,512]{1,0:T(8,128)S(1)} %get-tuple-element.97), channel_id=1, source_target_pairs={{0,4},{1,5},{2,6},{3,7},{4,8},{5,9},{6,10},{7,11},{8,12},{9,13},{1... | collective-permute-start | bytes 196616 | tf_op jit(solution)/shard_map/ppermute | solution.py:45
  568.2 12.6 %collective-permute-start.34 = (f32[32,512]{1,0:T(8,128)S(1)}, f32[32,512]{1,0:T(8,128)S(1)}, u32[]{:S(2)}, u32[]{:S(2)}) collective-permute-start(f32[32,512]{1,0:T(8,128)S(1)} %get-tuple-element.99), channel_id=1, source_target_pairs={{0,12},{1,13},{2,14},{3,15},{4,0},{5,1},{6,2},{7,3},{8,4},{9,5},{1... | collective-permute-start | bytes 196616 | tf_op jit(solution)/shard_map/ppermute | solution.py:45
  602.0 13.3 %collective-permute-start.57 = (f32[4,32,1024]{2,1,0:T(8,128)S(1)}, f32[4,32,1024]{2,1,0:T(8,128)S(1)}, u32[]{:S(2)}, u32[]{:S(2)}) collective-permute-start(f32[4,32,1024]{2,1,0:T(8,128)S(1)} %pad_maximum_fusion.17), channel_id=1, source_target_pairs={{0,4},{1,5},{2,6},{3,7},{4,8},{5,9},{6,10},{7,11},{8,12},{9,13},{1... | collective-permute-start | bytes 1572872 | tf_op jit(solution)/shard_map/ppermute | solution.py:45
  604.9 13.3 %collective-permute-start.41 = (f32[4,64,512]{2,1,0:T(8,128)S(1)}, f32[4,64,512]{2,1,0:T(8,128)S(1)}, u32[]{:S(2)}, u32[]{:S(2)}) collective-permute-start(f32[4,64,512]{2,1,0:T(8,128)S(1)} %pad_maximum_fusion.14), channel_id=1, source_target_pairs={{0,16},{1,17},{2,18},{3,19},{4,20},{5,21},{6,22},{7,23},{8,24},{9,... | collective-permute-start | bytes 1572872 | tf_op jit(solution)/shard_map/ppermute | solution.py:45
  607.0 19.5 %collective-permute-start.26 = (f32[256,1024]{1,0:T(8,128)S(1)}, f32[256,1024]{1,0:T(8,128)S(1)}, u32[]{:S(2)}, u32[]{:S(2)}) collective-permute-start(f32[256,1024]{1,0:T(8,128)S(1)} %dynamic-slice_add_fusion), channel_id=1, source_target_pairs={{0,2},{1,3},{2,0},{3,1},{4,6},{5,7},{6,4},{7,5},{8,10},{9,11},{10,... | collective-permute-start | bytes 3145736 | tf_op jit(solution)/shard_map/ppermute | solution.py:45
  (198 other events, 1441.3 us)
Sparse Core Ops, SparseCore 0:
  384.4 99.3 all-reduce.2

commit v2 on v1

v2 whole, which is shorter than its diff:
```python
import jax
import jax.numpy as jnp
from jax import lax
from jax.experimental import pallas as pl
from jax.experimental.pallas import tpu as pltpu
from jax.sharding import PartitionSpec as P

HEAD_DIM = 128
SEG = 512
RATE = 2
COMP = 256
CHUNK = 256
HALF = 128
QUARTER = 64
TILE = 256
BLOCK = 256
SUB = 64
HEADS = 2
SCALE = HEAD_DIM ** (-0.5)
LIMIT = 10 * 2**20
AXES = ("pipe", "dp", "tensor")


def pairs(move):
    found = []
    for p in range(2):
        for y in range(4):
            for z in range(4):
                for x in range(2):
                    for c in range(2):
                        there = move(p, y, z, x, c)
                        if there is None:
                            continue
                        q, v, w, u, d = there
                        source = ((p * 4 + y) * 4 + z) * 4 + x * 2 + c
                        target = ((q * 4 + v % 4) * 4 + w % 4) * 4 + u * 2 + d
                        found.append((source, target))
    return found


CORE = pairs(lambda p, y, z, x, c: (p, y, z, x, 1 - c))
CHIP = pairs(lambda p, y, z, x, c: (p, y, z, 1 - x, c))
CORE_FIRST = pairs(lambda p, y, z, x, c: (p, y, z, x, 1 - c) if p == 0 else None)
CHIP_FIRST = pairs(lambda p, y, z, x, c: (p, y, z, 1 - x, c) if p == 0 else None)
CORE_LAST = pairs(lambda p, y, z, x, c: (p, y, z, x, 1 - c) if p == 1 else None)
CHIP_LAST = pairs(lambda p, y, z, x, c: (p, y, z, 1 - x, c) if p == 1 else None)
ONWARD = pairs(lambda p, y, z, x, c: (1, y, z, 1 - x, c) if p == 0 else None)
BACK = pairs(lambda p, y, z, x, c: (0, y, z, 1 - x, c) if p == 1 else None)
Y_ONE = pairs(lambda p, y, z, x, c: (p, y ^ 1, z, x, c))
Y_TWO = pairs(lambda p, y, z, x, c: (p, y ^ 2, z, x, c))
Z_ONE = pairs(lambda p, y, z, x, c: (p, y, z ^ 1, x, c))
Z_TWO = pairs(lambda p, y, z, x, c: (p, y, z ^ 2, x, c))
UP = pairs(lambda p, y, z, x, c: (p, y + 1 - c, z + c, x, c))
DOWN = pairs(lambda p, y, z, x, c: (p, y + 3 * (1 - c), z + 3 * c, x, c))
UP2 = pairs(lambda p, y, z, x, c: (p, y + c, z + 1 - c, x, c))
DOWN2 = pairs(lambda p, y, z, x, c: (p, y + 3 * c, z + 3 * (1 - c), x, c))


def low(value):
    return value.astype(jnp.bfloat16)


def wide(value):
    return value.astype(jnp.float32)


def send(value, moves):
    return lax.ppermute(value, AXES, moves)


def after(value, anchor):
    return lax.optimization_barrier((value, anchor))[0]


def dot(left, right):
    return jnp.dot(left, right, preferred_element_type=jnp.float32)


def dot_t(left, right):
    return lax.dot_general(
        left, right, (((1,), (1,)), ((), ())), preferred_element_type=jnp.float32
    )


def t_dot(left, right):
    return lax.dot_general(
        left, right, (((0,), (0,)), ((), ())), preferred_element_type=jnp.float32
    )


def standardize(values):
    centered = values - jnp.mean(values, -1, keepdims=True)
    variance = jnp.mean(centered * centered, -1, keepdims=True)
    inverse = lax.rsqrt(variance + 1e-05)
    return centered * inverse, inverse


def standardize_back(grad, hat, inverse):
    return inverse * (
        grad
        - jnp.mean(grad, -1, keepdims=True)
        - hat * jnp.mean(grad * hat, -1, keepdims=True)
    )


def gelu_and_slope(value):
    square = value * value
    curve = jnp.tanh(0.7978845608028654 * value * (1.0 + 0.044715 * square))
    up = 0.5 + 0.5 * curve
    slope = up + (0.5 * value) * (1.0 - curve * curve) * (
        0.7978845608028654 + (3 * 0.044715 * 0.7978845608028654) * square
    )
    return value * up, slope


F32, BF16 = jnp.float32, jnp.bfloat16
WHOLE = pl.BlockSpec(memory_space=pltpu.VMEM)
SCALAR = pl.BlockSpec(memory_space=pltpu.SMEM)
ANYWHERE = pl.BlockSpec(memory_space=pl.ANY)
OUTSIDE = pl.BlockSpec(memory_space=pltpu.HBM)
CORE_AT, ON_AT, BACK_AT, FIRST_AT, RING_AT, RING2_AT, MEMBER_AT = range(7)


class Order:
    def __init__(self, flags):
        self.flags = flags

    def then(self, anchor):
        self.flags = after(self.flags, anchor)

    def call(self, kernel, outs, args, flops=1, scratch=(), specs=None, out_specs=None, aliases=None):
        args = [self.flags, *args]
        results = pl.pallas_call(
            kernel,
            out_shape=[jax.ShapeDtypeStruct(shape, dtype) for shape, dtype in outs],
            in_specs=[SCALAR] + (specs or [WHOLE] * (len(args) - 1)),
            out_specs=out_specs or [WHOLE] * len(outs),
            scratch_shapes=list(scratch),
            input_output_aliases=aliases or {},
            compiler_params=pltpu.CompilerParams(vmem_limit_bytes=LIMIT),
            cost_estimate=pl.CostEstimate(flops=1, bytes_accessed=1, transcendentals=0),
        )(*args)
        self.then(results[0])
        return results


def at_rows(index, size):
    return pl.ds(pl.multiple_of(index * size, size), size)


def put_pieces(out_ref, pieces, core, place, start=0):
    spots = (
        core * 2 + place,
        core * 2 + 1 - place,
        (1 - core) * 2 + place,
        (1 - core) * 2 + 1 - place,
    )
    for piece, spot in zip(pieces, spots):
        out_ref[at_rows(spot + start // QUARTER, QUARTER), :] = piece[...]


def halves_of(width):
    return [((HALF, width), F32)] + [((QUARTER, width), F32)] * 2


def split_halves(value_ref, own_ref, send_refs, core):
    own_ref[...] = value_ref[at_rows(core, HALF), :]
    for i, ref in enumerate(send_refs):
        ref[...] = value_ref[at_rows(2 * (1 - core) + i, QUARTER), :]


def put_halves(out_ref, own, others, core):
    out_ref[at_rows(core, HALF), :] = own[...]
    for i, ref in enumerate(others):
        out_ref[at_rows(2 * (1 - core) + i, QUARTER), :] = ref[...]


def chunk_rows(index):
    return slice(index * CHUNK, (index + 1) * CHUNK)


def row_documents(docs, start):
    row = lax.broadcasted_iota(jnp.int32, (CHUNK, CHUNK), 0)
    col = lax.broadcasted_iota(jnp.int32, (CHUNK, CHUNK), 1)
    own = wide(docs[:, start : start + CHUNK])
    return jnp.sum(jnp.where(row == col, own, 0.0), -1, keepdims=True)


def masked(scores, docs_q, docs_k, causal):
    allowed = docs_q == docs_k
    if causal:
        q_pos = lax.broadcasted_iota(jnp.int32, scores.shape, 0)
        k_pos = lax.broadcasted_iota(jnp.int32, scores.shape, 1)
        allowed = allowed & (k_pos <= q_pos)
    return jnp.where(allowed, scores * SCALE, -1e30)


def prepare_memory(order, older, memory, gain, shift, key_w, value_w):
    held, width = older.shape[0] + memory.shape[0], older.shape[1]
    local = key_w.shape[1]
    pieces = range(0, held, CHUNK)

    def kernel(flag, older_ref, memory_ref, *refs):
        outside, (normed, k, v), refs = refs[:4], refs[4:7], refs[7:]
        gain_ref, shift_ref, wk, wv, rows_ref, sems = refs
        copies = [
            pltpu.make_async_copy(source, target, sems.at[i])
            for i, (source, target) in enumerate(zip(outside, (gain_ref, shift_ref, wk, wv)))
        ]
        for start in pieces:
            source = older_ref if start < older.shape[0] else memory_ref
            at = start % older.shape[0]
            copies.append(
                pltpu.make_async_copy(
                    source.at[at : at + CHUNK, :],
                    rows_ref.at[start : start + CHUNK, :],
                    sems.at[len(copies)],
                )
            )
        for copy in copies:
            copy.start()
        copies[0].wait()
        copies[1].wait()
        gain_row, shift_row = wide(gain_ref[...]), wide(shift_ref[...])
        for i, start in enumerate(pieces):
            copies[4 + i].wait()
            at = slice(start, start + CHUNK)
            hat, _ = standardize(wide(rows_ref[at, :]))
            normed[at, :] = low(hat * gain_row + shift_row)
            if i == 0:
                copies[2].wait()
                copies[3].wait()
            k[at, :] = low(dot(normed[at, :], wk[...]))
            v[at, :] = low(dot(normed[at, :], wv[...]))

    outs = [((held, width), BF16), ((held, local), BF16), ((held, local), BF16)]
    args = [older, memory, gain, shift, key_w, value_w]
    scratch = [pltpu.VMEM(a.shape, BF16) for a in args[2:]]
    scratch += [pltpu.VMEM((held, width), BF16), pltpu.SemaphoreType.DMA((4 + len(pieces),))]
    return order.call(kernel, outs, args, 1, scratch, specs=[OUTSIDE] * len(args))


def attend_chunk(order, inputs, pieces, past, docs, index, weights, gain, shift, output_w, keep):
    given, held = len(pieces), [k.shape[0] for k, _ in past]
    starts = [sum(held[:i]) for i in range(len(held) + 1)]

    def kernel(*refs):
        flag, x_in = refs[0], refs[1]
        piece_refs, rest = refs[2 : 2 + given], refs[2 + given :]
        gain_ref, shift_ref, wq, wk, wv, docs_ref, wo = rest[:7]
        past_refs, rest = rest[7 : 7 + 2 * len(held)], rest[7 + 2 * len(held) :]
        if keep:
            x, k, v, own, *others, hat, inverse, normed, q, lse, mixed, acc = rest
        else:
            x, k, v, own, *others, normed, q, mixed, acc = rest
        if given:
            put_pieces(x, piece_refs, flag[CORE_AT], flag[ON_AT])
            x[...] = jnp.where(flag[FIRST_AT] == 1, wide(x_in[chunk_rows(index), :]), x[...])
        else:
            x[...] = wide(x_in[chunk_rows(index), :])
        hat_value, inverse_value = standardize(x[...])
        normed[...] = low(hat_value * wide(gain_ref[...]) + wide(shift_ref[...]))
        if keep:
            hat[...], inverse[...] = hat_value, inverse_value
        q[...] = low(dot(normed[...], wq[...]))
        k[...] = low(dot(normed[...], wk[...]))
        v[...] = low(dot(normed[...], wv[...]))
        parts = [(past_refs[2 * i], past_refs[2 * i + 1]) for i in range(len(held))] + [(k, v)]
        sizes = held + [CHUNK]
        docs_q = row_documents(docs_ref, starts[-1])
        for h in range(HEADS):
            cols = slice(h * HEAD_DIM, (h + 1) * HEAD_DIM)
            scores = [
                masked(
                    dot_t(q[:, cols], key[:, cols]),
                    docs_q,
                    wide(docs_ref[:, start : start + size]),
                    key is k,
                )
                for (key, _), start, size in zip(parts, starts, sizes)
            ]
            top = scores[0].max(-1, keepdims=True)
            for score in scores[1:]:
                top = jnp.maximum(top, score.max(-1, keepdims=True))
            total, out = 0.0, 0.0
            for score, (_, value) in zip(scores, parts):
                exps = jnp.exp(score - top)
                total = total + exps.sum(-1, keepdims=True)
                out = out + dot(low(exps), value[:, cols])
            if keep:
                lse[:, h : h + 1] = top + jnp.log(total)
            mixed[:, cols] = low(out / total)
        acc[...] = dot(mixed[...], wo[...])
        split_halves(acc, own, others, flag[CORE_AT])

    width, local = inputs.shape[1], weights[0].shape[1]
    size = starts[-1] + CHUNK
    outs = [((CHUNK, width), F32), ((CHUNK, local), BF16), ((CHUNK, local), BF16)]
    outs += halves_of(width)
    kept = [
        ((CHUNK, width), F32),
        ((CHUNK, 1), F32),
        ((CHUNK, width), BF16),
        ((CHUNK, local), BF16),
        ((CHUNK, HEADS), F32),
        ((CHUNK, local), BF16),
    ]
    if keep:
        outs, scratch = outs + kept, []
    else:
        scratch = [pltpu.VMEM(*kept[i]) for i in (2, 3, 5)]
    args = [inputs, *pieces, gain, shift, *weights, docs, output_w]
    args += [item for pair in past for item in pair]
    return order.call(kernel, outs, args, 1, scratch + [pltpu.VMEM((CHUNK, width), F32)])


def feed_chunk(order, layer_input, parts, output_b, gain, shift, inner_w, inner_b, outer_w):
    ending = outer_w is not None
    units = inner_w.shape[1]

    def kernel(flag, x, half, twin0, twin1, bo, gain_ref, shift_ref, wi, bi, *rest):
        if ending:
            wf, hidden, own, *others, acc = rest
        else:
            hidden, hat_ref, inverse_ref, normed_ref, acts_ref, slope_ref = rest
        put_halves(hidden, half, (twin0, twin1), flag[CORE_AT])
        hidden[...] = x[...] + (hidden[...] + wide(bo[...]))
        hat, inverse = standardize(hidden[...])
        normed = low(hat * wide(gain_ref[...]) + wide(shift_ref[...]))
        if not ending:
            hat_ref[...], inverse_ref[...], normed_ref[...] = hat, inverse, normed
        for start in range(0, units, TILE):
            tile = slice(start, start + TILE)
            acts, slope = gelu_and_slope(dot(normed, wi[:, tile]) + wide(bi[:, tile]))
            if ending:
                term = dot(low(acts), wf[tile, :])
                acc[...] = term if start == 0 else acc[...] + term
            else:
                acts_ref[:, tile] = low(acts)
                slope_ref[:, tile] = slope
        if ending:
            split_halves(acc, own, others, flag[CORE_AT])

    width = layer_input.shape[1]
    outs = [((CHUNK, width), F32)]
    if ending:
        outs += halves_of(width)
    else:
        outs += [
            ((CHUNK, width), F32),
            ((CHUNK, 1), F32),
            ((CHUNK, width), BF16),
            ((CHUNK, units), BF16),
            ((CHUNK, units), F32),
        ]
    args = [layer_input, *parts, output_b, gain, shift, inner_w, inner_b]
    args += [outer_w] if ending else []
    scratch = [pltpu.VMEM((CHUNK, width), F32)] if ending else []
    return order.call(kernel, outs, args, 1, scratch)


def feed_back_chunk(order, cotangent, index, pieces, kept, outer_w, inner_w, final):
    hat, slope = kept
    given, units = len(pieces), outer_w.shape[0]

    def kernel(*refs):
        flag, cot = refs[0], refs[1]
        piece_refs, rest = refs[2 : 2 + given], refs[2 + given :]
        slope_ref, wf, wi = rest[:3]
        if final:
            hat_ref, grad_out, own, *others, branch, pre_grad, sums, acc = rest[3:]
        else:
            grad_out, own, *others, acc = rest[3:]
        own_cot = wide(cot[chunk_rows(index), :])
        if given:
            put_pieces(grad_out, piece_refs, flag[CORE_AT], flag[BACK_AT])
            grad_out[...] = jnp.where(flag[FIRST_AT] == 1, grad_out[...], own_cot)
        else:
            grad_out[...] = own_cot
        branch_grad = low(grad_out[...])
        for start in range(0, units, TILE):
            tile = slice(start, start + TILE)
            grad = low(slope_ref[:, tile] * dot_t(branch_grad, wf[tile, :]))
            if final:
                pre_grad[:, tile] = grad
                sums[3:4, tile] = jnp.sum(wide(grad), 0, keepdims=True)
            term = dot_t(grad, wi[:, tile])
            acc[...] = term if start == 0 else acc[...] + term
        split_halves(acc, own, others, flag[CORE_AT])
        if final:
            branch[...] = branch_grad
            sums[0:1, :] = jnp.sum(acc[...] * hat_ref[...], 0, keepdims=True)
            sums[1:2, :] = jnp.sum(acc[...], 0, keepdims=True)
            sums[2:3, :] = jnp.sum(wide(branch_grad), 0, keepdims=True)

    width = cotangent.shape[1]
    outs = [((CHUNK, width), F32)] + halves_of(width)
    args = [cotangent, *pieces, slope, outer_w, inner_w]
    if final:
        outs += [((CHUNK, width), BF16), ((CHUNK, units), BF16), ((4, width), F32)]
        args += [hat]
    flops = 4 * CHUNK * width * units
    return order.call(kernel, outs, args, flops, [pltpu.VMEM((CHUNK, width), F32)])


def attend_back_chunk(
    order, grad_out, parts, kept_f, kept_a, past, docs, weights, gain_f, later, final
):
    hat_f, inverse_f = kept_f
    hat, queries, keys, values, lse = kept_a
    held = [k.shape[0] for k, _ in past]
    starts = [sum(held[:i]) for i in range(len(held) + 1)]
    sizes = held + [CHUNK]
    last = len(held) > 1
    width, local = hat.shape[1], queries.shape[1]
    size = starts[-1] + CHUNK

    def kernel(*refs):
        refs = list(refs)

        def take(count):
            taken = refs[:count]
            del refs[:count]
            return taken

        flag, g_out, half, twin0, twin1, hf, invf, gf, wo, wq, wk, wv, docs_ref = take(13)
        q, k, v, lse_ref = take(4)
        past_refs = take(2 * len(held))
        later_refs = take(len(later))
        hat_ref = take(1)[0] if final else None
        hidden_grad, own, *others = take(4)
        passed = take(2) if last else []
        kept = take(7) if final else []
        acc, key_acc, value_acc = take(3)
        core = flag[CORE_AT]
        put_halves(acc, half, (twin0, twin1), core)
        grad = standardize_back(acc[...] * wide(gf[...]), hf[...], invf[...])
        hidden_grad[...] = g_out[...] + grad
        attend_grad = low(hidden_grad[...])
        mixed_grad = low(dot_t(attend_grad, wo[...]))
        parts = [(past_refs[2 * i], past_refs[2 * i + 1]) for i in range(len(held))] + [(k, v)]
        query_rows = []
        docs_q = row_documents(docs_ref, starts[-1])
        for h in range(HEADS):
            cols = slice(h * HEAD_DIM, (h + 1) * HEAD_DIM)
            grad = mixed_grad[:, cols]
            probs, probs_grads, inner = [], [], 0.0
            for (key, value), start, length in zip(parts, starts, sizes):
                score = masked(
                    dot_t(q[:, cols], key[:, cols]),
                    docs_q,
                    wide(docs_ref[:, start : start + length]),
                    key is k,
                )
                probs.append(jnp.exp(score - lse_ref[:, h : h + 1]))
                probs_grads.append(dot_t(grad, value[:, cols]))
                inner = inner + jnp.sum(probs[-1] * probs_grads[-1], -1, keepdims=True)
            query_row = 0.0
            for i, (key, value) in enumerate(parts):
                score_grad = low(probs[i] * (probs_grads[i] - inner))
                query_row = query_row + dot(score_grad, key[:, cols])
                if i == 0 and not final:
                    continue
                key_sum = t_dot(score_grad, q[:, cols])
                value_sum = t_dot(low(probs[i]), grad)
                key_acc[starts[i] : starts[i] + sizes[i], cols] = key_sum
                value_acc[starts[i] : starts[i] + sizes[i], cols] = value_sum
            query_rows.append(low(query_row * SCALE))
        query_rows = jnp.concatenate(query_rows, 1)
        key_own, value_own = key_acc[starts[-1] : size, :], value_acc[starts[-1] : size, :]
        if last:
            passed[0][...] = key_acc[starts[1] : starts[2], :]
            passed[1][...] = value_acc[starts[1] : starts[2], :]
        else:
            key_own, value_own = key_own + later_refs[0][...], value_own + later_refs[1][...]
        key_rows, value_rows = low(key_own * SCALE), low(value_own)
        acc[...] = dot_t(query_rows, wq[...]) + dot_t(key_rows, wk[...])
        acc[...] = acc[...] + dot_t(value_rows, wv[...])
        split_halves(acc, own, others, core)
        if final:
            kept[0][...], kept[1][...] = query_rows, key_rows
            kept[2][...], kept[3][...] = value_rows, attend_grad
            memory_key, memory_value = key_acc[: held[0], :], value_acc[: held[0], :]
            if last:
                kept[4][...], kept[5][...] = memory_key, memory_value
            else:
                kept[4][...] = low((memory_key + later_refs[2][...]) * SCALE)
                kept[5][...] = low(memory_value + later_refs[3][...])
            sums = kept[6]
            sums[0:1, :] = jnp.sum(acc[...] * hat_ref[...], 0, keepdims=True)
            sums[1:2, :] = jnp.sum(acc[...], 0, keepdims=True)
            sums[2:3, :] = jnp.sum(wide(attend_grad), 0, keepdims=True)
            sums[3:4, :] = jnp.zeros_like(sums[3:4, :])

    outs = [((CHUNK, width), F32)] + halves_of(width)
    if last:
        outs += [((CHUNK, local), F32)] * 2
    if final:
        outs += [((CHUNK, local), BF16)] * 3 + [((CHUNK, width), BF16)]
        outs += [((held[0], local), F32 if last else BF16)] * 2 + [((4, width), F32)]
    args = [grad_out, *parts, hat_f, inverse_f, gain_f, *weights, docs]
    args += [queries, keys, values, lse] + [item for pair in past for item in pair] + list(later)
    args += [hat] if final else []
    scratch = [
        pltpu.VMEM((CHUNK, width), F32),
        pltpu.VMEM((size, local), F32),
        pltpu.VMEM((size, local), F32),
    ]
    flops = 2 * CHUNK * local * (4 * width + 5 * size)
    return order.call(kernel, outs, args, flops, scratch)


def add(order, *terms):
    def kernel(flag, *refs):
        total = refs[0][...]
        for ref in refs[1:-1]:
            total = total + ref[...]
        refs[-1][...] = total

    return order.call(kernel, [(terms[0].shape, F32)], terms)[0]


def add_pieces(order, own, pieces):
    def kernel(flag, a, b0, b1, out):
        out[:QUARTER, :] = a[:QUARTER, :] + b0[...]
        out[QUARTER:, :] = a[QUARTER:, :] + b1[...]

    return order.call(kernel, [(own.shape, F32)], [own, *pieces])[0]


def add_into_pieces(order, own, arrived):
    def kernel(flag, a, b, out, first, second):
        out[...] = a[...] + b[...]
        first[...], second[...] = out[:QUARTER, :], out[QUARTER:, :]

    return order.call(kernel, halves_of(own.shape[1]), [own, arrived])


def halve(order, own, arrived, place_at):
    def kernel(flag, a, b0, b1, mine, other):
        place = flag[place_at]
        mine[...] = a[at_rows(place, QUARTER), :] + jnp.where(place == 0, b0[...], b1[...])
        other[...] = a[at_rows(1 - place, QUARTER), :] + jnp.where(place == 0, b1[...], b0[...])

    return order.call(kernel, [((QUARTER, own.shape[1]), F32)] * 2, [own, *arrived])


def finish_forward(order, mine, arrived, hidden, outer_b):
    def kernel(flag, a, b, h, bias, out):
        at = at_rows(flag[CORE_AT] * 2 + flag[ON_AT], QUARTER)
        out[...] = a[...] + b[...] + h[at, :] + wide(bias[...])

    return order.call(kernel, [(mine.shape, F32)], [mine, arrived, hidden, outer_b])[0]


def finish_backward(order, mine, arrived, hat, inverse, hidden_grad, gain):
    def kernel(flag, a, b, hat_ref, inverse_ref, h, gain_ref, out):
        at = at_rows(flag[CORE_AT] * 2 + flag[BACK_AT], QUARTER)
        grad = (a[...] + b[...]) * wide(gain_ref[...])
        out[...] = h[at, :] + standardize_back(grad, hat_ref[at, :], inverse_ref[at, :])

    args = [mine, arrived, hat, inverse, hidden_grad, gain]
    return order.call(kernel, [(mine.shape, F32)], args)[0]


def pick(order, arrived, own, receiver):
    def kernel(flag, a, b, out):
        out[...] = jnp.where(flag[FIRST_AT] == receiver, a[...], b[...])

    return order.call(kernel, [(own.shape, F32)], [arrived, own])[0]


def squeeze(order, memory, older, weight, bias):
    local = weight.shape[-1]

    def kernel(flag, memory_ref, older_ref, w, b, out):
        row = lax.broadcasted_iota(jnp.int32, (COMP, memory.shape[0]), 0)
        col = lax.broadcasted_iota(jnp.int32, (COMP, memory.shape[0]), 1)
        total = wide(b[...])
        for r in range(RATE):
            chosen = low(wide((col == row * RATE + r).astype(jnp.int32)))
            total = total + dot(low(dot(chosen, memory_ref[...])), w[r])
        out[:COMP, :] = older_ref[COMP:, at_rows(flag[MEMBER_AT], local)]
        out[COMP:, :] = low(total)

    return order.call(kernel, [((2 * COMP, local), BF16)], [memory, older, weight, bias])[0]


def memory_sums(order, older, memory, keys_grad, values_grad, key_w, value_w):
    def kernel(flag, older_ref, memory_ref, kg, vg, wk, wv, out):
        out[...] = jnp.zeros_like(out)
        for i, source in enumerate((older_ref, memory_ref)):
            for start in range(0, source.shape[0], CHUNK):
                hat, _ = standardize(wide(source[start : start + CHUNK, :]))
                at = slice(i * source.shape[0] + start, i * source.shape[0] + start + CHUNK)
                grad = dot_t(kg[at, :], wk[...]) + dot_t(vg[at, :], wv[...])
                out[0:1, :] = out[0:1, :] + jnp.sum(grad * hat, 0, keepdims=True)
                out[1:2, :] = out[1:2, :] + jnp.sum(grad, 0, keepdims=True)

    width, local = key_w.shape
    args = [older, memory, keys_grad, values_grad, key_w, value_w]
    flops = 4 * (older.shape[0] + memory.shape[0]) * width * local
    return order.call(kernel, [((2, width), F32)], args, flops)[0]


def block_at(index):
    return at_rows(index % 4, BLOCK)


def sub_at(index):
    return at_rows(index % 4, SUB)


def ring_sum(order, operands, make, columns, outs, place, extra=None):
    more = 0 if extra is None else extra.shape[0]
    extras = [] if extra is None else [extra]

    def rows_of(count, added=0):
        return ((count + added, columns), F32)

    blocks = [pltpu.VMEM((2, BLOCK, columns), F32)]

    def both(upward, up_moves, downward, down_moves):
        upward, downward = after((upward, downward), order.flags)
        return send(upward, up_moves), send(downward, down_moves)

    def far_kernel(flag, *refs):
        for q in range(2):
            refs[-2 + q][:BLOCK, :] = make(refs, q, flag[RING_AT] + 2)
            if more:
                refs[-2 + q][BLOCK:, :] = refs[-3][...]

    far = order.call(far_kernel, [rows_of(BLOCK, more)] * 2, operands + extras)
    yield
    below, above = both(far[0], UP, far[1], DOWN)
    yield

    def next_kernel(flag, *refs):
        below_ref, above_ref, up_ref, down_ref = refs[-4:]
        here = flag[RING_AT]
        up_ref[:BLOCK, :] = make(refs, 0, here + 1) + below_ref[:BLOCK, :]
        up_ref[BLOCK : 2 * BLOCK, :] = make(refs, 1, here + 1)
        down_ref[:BLOCK, :] = make(refs, 0, here + 3)
        down_ref[BLOCK : 2 * BLOCK, :] = make(refs, 1, here + 3) + above_ref[:BLOCK, :]
        if more:
            up_ref[2 * BLOCK :, :] = below_ref[BLOCK:, :]
            down_ref[2 * BLOCK :, :] = refs[-5][...] + below_ref[BLOCK:, :] + above_ref[BLOCK:, :]

    up, down = order.call(
        next_kernel, [rows_of(2 * BLOCK, more)] * 2, [*operands, *extras, below, above]
    )
    extras = [down] if more else []
    yield
    below, above = both(up, UP, down, DOWN)
    yield

    def own_kernel(flag, *refs):
        below_ref, above_ref, far_p, far_q, up_ref, down_ref, own_ref, acc = refs[-8:]
        if more:
            partial = refs[-9][2 * BLOCK :, :] + below_ref[2 * BLOCK :, :]
            far_p[SUB:, :], far_q[SUB:, :] = partial, partial
            up_ref[2 * SUB :, :], down_ref[2 * SUB :, :] = partial, partial
        here, there = flag[RING_AT], flag[RING2_AT]
        for q in range(2):
            at = slice(q * BLOCK, (q + 1) * BLOCK)
            acc[q] = make(refs, q, here) + below_ref[at, :] + above_ref[at, :]
            half = slice(q * SUB, (q + 1) * SUB)
            (far_p, far_q)[q][:SUB, :] = acc[q, sub_at(there + 2), :]
            up_ref[half, :] = acc[q, sub_at(there + 1), :]
            down_ref[half, :] = acc[q, sub_at(there + 3), :]
            own_ref[half, :] = acc[q, sub_at(there), :]

    far_p, far_q, up, down, own = order.call(
        own_kernel,
        [rows_of(SUB, more)] * 2 + [rows_of(2 * SUB, more)] * 2 + [rows_of(2 * SUB)],
        [*operands, *extras, below, above],
        scratch=blocks,
    )
    yield
    below, above = both(far_p, UP2, far_q, DOWN2)
    yield

    def next_small(flag, up_in, down_in, below_ref, above_ref, up_ref, down_ref):
        p, q, rest = slice(0, SUB), slice(SUB, 2 * SUB), slice(2 * SUB, None)
        up_ref[p, :], up_ref[q, :] = up_in[p, :] + below_ref[:SUB, :], up_in[q, :]
        down_ref[p, :], down_ref[q, :] = down_in[p, :], down_in[q, :] + above_ref[:SUB, :]
        if more:
            up_ref[rest, :] = below_ref[SUB:, :]
            down_ref[rest, :] = down_in[rest, :] + below_ref[SUB:, :] + above_ref[SUB:, :]

    up, down = order.call(
        next_small, [rows_of(2 * SUB, more)] * 2, [up, down, below, above]
    )
    yield
    below, above = both(up, UP2, down, DOWN2)
    yield

    def own_small(flag, own_ref, below_ref, above_ref, down_ref, out, *rest):
        out[...] = own_ref[...] + below_ref[: 2 * SUB, :] + above_ref[: 2 * SUB, :]
        if more:
            rest[0][...] = down_ref[2 * SUB :, :] + below_ref[2 * SUB :, :]

    outs_small = [rows_of(2 * SUB)] + ([rows_of(more)] if more else [])
    own, *extras = order.call(own_small, outs_small, [own, below, above, down])
    yield extras
    below, above = both(own, UP2, own, DOWN2)
    yield

    def pass_small(flag, below_ref, above_ref, up_ref, down_ref):
        up_ref[...], down_ref[...] = below_ref[:SUB, :], above_ref[SUB:, :]

    up, down = order.call(pass_small, [rows_of(SUB)] * 2, [below, above])
    yield
    far_p, far_q = both(up, UP2, down, DOWN2)
    yield

    def join(flag, own_ref, below_ref, above_ref, far_p_ref, far_q_ref, out, acc):
        there = flag[RING2_AT]
        for q, far_ref in enumerate((far_p_ref, far_q_ref)):
            half = slice(q * SUB, (q + 1) * SUB)
            acc[q, sub_at(there), :] = own_ref[half, :]
            acc[q, sub_at(there + 3), :] = below_ref[half, :]
            acc[q, sub_at(there + 1), :] = above_ref[half, :]
            acc[q, sub_at(there + 2), :] = far_ref[...]
            out[q * BLOCK : (q + 1) * BLOCK, :] = acc[q]

    total = order.call(
        join, [rows_of(2 * BLOCK)], [own, below, above, far_p, far_q], 1, blocks
    )[0]
    yield
    below, above = both(total, UP, total, DOWN)
    yield

    def pass_kernel(flag, below_ref, above_ref, up_ref, down_ref):
        up_ref[...], down_ref[...] = below_ref[:BLOCK, :], above_ref[BLOCK:, :]

    up, down = order.call(pass_kernel, [rows_of(BLOCK)] * 2, [below, above])
    yield
    far_p, far_q = both(up, UP, down, DOWN)
    yield

    copies = len(place(0, 0)) + len(place(1, 0))

    def run(moves, sems):
        started = [pltpu.make_async_copy(a, b, sems.at[i]) for i, (a, b) in enumerate(moves)]
        for copy in started:
            copy.start()
        for copy in started:
            copy.wait()

    def moves_of(piece, start, q, index, out_refs):
        return [
            (piece.at[start : start + BLOCK, cols], out_refs[out].at[to])
            for cols, out, to in place(q, index)
        ]

    def first_writes(flag, own_ref, below_ref, above_ref, *rest):
        out_refs, sems = rest[:-1], rest[-1]
        here = flag[RING_AT]
        moves = []
        for piece, index in ((own_ref, here), (below_ref, here + 3), (above_ref, here + 1)):
            for q in range(2):
                moves += moves_of(piece, q * BLOCK, q, index, out_refs)
        run(moves, sems)

    outs = [(shape, F32) for shape in outs]
    results = order.call(
        first_writes,
        outs,
        [total, below, above],
        1,
        [pltpu.SemaphoreType.DMA((3 * copies,))],
        out_specs=[ANYWHERE] * len(outs),
    )
    yield

    def last_writes(flag, far_p_ref, far_q_ref, *rest):
        out_refs, sems = rest[len(outs) : -1], rest[-1]
        index = flag[RING_AT] + 2
        moves = moves_of(far_p_ref, 0, 0, index, out_refs)
        moves += moves_of(far_q_ref, 0, 1, index, out_refs)
        run(moves, sems)

    results = order.call(
        last_writes,
        outs,
        [far_p, far_q, *results],
        1,
        [pltpu.SemaphoreType.DMA((copies,))],
        specs=[WHOLE] * 2 + [ANYWHERE] * len(outs),
        out_specs=[ANYWHERE] * len(outs),
        aliases={3 + i: i for i in range(len(outs))},
    )
    return [*results, *extras]


class Task:
    def __init__(self, steps):
        self.steps, self.result, self.ended, self.extra = steps, None, False, None

    def step(self, count=1):
        for _ in range(count):
            if not self.ended:
                try:
                    told = next(self.steps)
                    self.extra = told[0] if told else self.extra
                except StopIteration as end:
                    self.result, self.ended = end.value, True
        return self.result

    def finish(self):
        while not self.ended:
            self.step()
        return self.result


def body(
    inputs,
    memories,
    compressed,
    documents,
    cotangent,
    compressed_cotangent,
    query_weight,
    key_weight,
    value_weight,
    output_weight,
    output_bias,
    inner_weight,
    inner_bias,
    outer_weight,
    outer_bias,
    conv_weight,
    conv_bias,
    attn_gain,
    attn_shift,
    ffn_gain,
    ffn_shift,
):
    section = lax.axis_index("pipe")
    group = lax.axis_index("dp")
    member = lax.axis_index("tensor")
    core, chip = member % 2, member // 2
    on_place = jnp.where(section == 0, chip, 1 - chip)
    y, z = group // 4, group % 4
    ring, ring2 = jnp.where(core == 0, y, z), jnp.where(core == 0, z, y)
    order = Order(
        jnp.stack([core, on_place, 1 - on_place, 1 - section, ring, ring2, member]).astype(jnp.int32)
    )
    width = inputs.shape[1]
    local = query_weight.shape[2]
    held = documents.shape[1] - SEG
    chunks = range(SEG // CHUNK)
    qkv_w = (query_weight[0], key_weight[0], value_weight[0])
    key_w, value_w, output_w = key_weight[0], value_weight[0], output_weight[0]
    inner_w, outer_w = inner_weight[0], outer_weight[0]
    norm_a, norm_f = (attn_gain, attn_shift), (ffn_gain, ffn_shift)
    memory, older = memories[0, 0], compressed[0, 0]
    squeeze_cot = compressed_cotangent[0, 0]

    memory_low, *past_memory = prepare_memory(order, older, memory, *norm_a, key_w, value_w)

    def make_conv(refs, q, index):
        memory_ref, cot = refs[:2]
        row = lax.broadcasted_iota(jnp.int32, (SEG, COMP), 0)
        col = lax.broadcasted_iota(jnp.int32, (SEG, COMP), 1)
        chosen = low(wide((row == col * RATE + q).astype(jnp.int32)))
        return t_dot(memory_ref[:, block_at(index)], low(dot(chosen, cot[...])))

    def place_conv(q, index):
        return [(slice(None), 0, (q, block_at(index)))]

    conv = Task(
        ring_sum(order, [memory, squeeze_cot], make_conv, local, [(RATE, width, local)], place_conv)
    )

    weights_a = (qkv_w, *norm_a, output_w)
    weights_f = (output_bias, *norm_f, inner_w, inner_bias)

    def twins(pieces, moves):
        return [send(piece, moves) for piece in pieces]

    def to_chip(own, pieces, moves):
        total = add_pieces(order, own, pieces)
        return total, send(total, moves)

    def to_core(value, arrived, moves):
        total, *pieces = add_into_pieces(order, value, arrived)
        return [total, *twins(pieces, moves)]

    def spread(piece):
        beyond = send(piece, CHIP)
        return [piece, beyond, send(piece, CORE), send(beyond, CORE)]

    attended, past = [], [past_memory]
    for i in chunks:
        made = attend_chunk(order, inputs, [], past, documents, i, *weights_a, False)
        past = past + [(made[1], made[2])]
        attended.append((made[0], made[3], twins(made[4:], CORE_FIRST)))

    def feed(i, parts):
        hidden, own, *others = feed_chunk(order, attended[i][0], parts, *weights_f, outer_w)
        return hidden, own, twins(others, CORE_FIRST)

    def split(own, arrived):
        mine, other = halve(order, own, arrived, ON_AT)
        return mine, send(other, CHIP_FIRST)

    def finish(hidden, mine, arrived):
        total = finish_forward(order, mine, arrived, hidden, outer_bias)
        return send(total, ONWARD), total

    half0 = to_chip(*attended[0][1:], CHIP_FIRST)
    half1 = to_chip(*attended[1][1:], CHIP_FIRST)
    conv.step(4)
    half0 = to_core(*half0, CORE_FIRST)
    hidden0, *half0 = feed(0, half0)
    quarter0 = split(*half0)
    half1 = to_core(*half1, CORE_FIRST)
    conv.step(2)
    total0 = finish(hidden0, *quarter0)
    hidden1, *half1 = feed(1, half1)
    quarter1 = split(*half1)
    conv.step(2)
    total1 = finish(hidden1, *quarter1)

    forward, kept_a, kept_f, pasts = [], [], [], [[past_memory]]

    def attend(i):
        made = attend_chunk(order, inputs, forward[i], pasts[i], documents, i, *weights_a, True)
        kept_a.append(made)
        pasts.append(pasts[i] + [(made[1], made[2])])
        return made[3], twins(made[4:6], CORE)

    def feed_last(i, parts):
        kept_f.append(feed_chunk(order, kept_a[i][0], parts, *weights_f, None))

    def feed_back(i, pieces, final, core_moves):
        made = feed_back_chunk(
            order, cotangent, i, pieces, (kept_f[i][1], kept_f[i][5]), outer_w, inner_w, final
        )
        return made, (made[1], twins(made[2:4], core_moves))

    def attend_back(i, grad_out, parts, later, final):
        x, k, v, _, _, _, hat, inverse, normed, q, lse, mixed = kept_a[i]
        return attend_back_chunk(
            order,
            grad_out,
            parts,
            kept_f[i][1:3],
            (hat, q, k, v, lse),
            pasts[i],
            documents,
            (output_w, *qkv_w),
            ffn_gain,
            later,
            final,
        )

    forward.append(spread(pick(order, *total0, 0)))
    conv.step(2)
    half0 = attend(0)
    forward.append(spread(pick(order, *total1, 0)))
    half0 = to_chip(*half0, CHIP)
    half1 = attend(1)
    half1 = to_chip(*half1, CHIP)
    conv.step(4)
    half0 = to_core(*half0, CORE)
    feed_last(0, half0)
    made0, half0 = feed_back(0, [], False, CORE_LAST)
    half0 = to_chip(*half0, CHIP_LAST)
    half1 = to_core(*half1, CORE)
    feed_last(1, half1)
    made1, half1 = feed_back(1, [], False, CORE_LAST)
    half1 = to_chip(*half1, CHIP_LAST)
    conv.step(2)
    half0 = to_core(*half0, CORE_LAST)
    half1 = to_core(*half1, CORE_LAST)

    def split_back(own, others):
        mine, other = halve(order, own, others, BACK_AT)
        return mine, send(other, CHIP_LAST)

    def finish_back(i, made, mine, arrived):
        total = finish_backward(
            order, mine, arrived, kept_a[i][6], kept_a[i][7], made[0], attn_gain
        )
        return send(total, BACK), total

    back1 = attend_back(1, made1[0], half1, [], False)
    half1 = back1[1], twins(back1[2:4], CORE_LAST)
    back0 = attend_back(0, made0[0], half0, back1[4:6], False)
    half0 = back0[1], twins(back0[2:4], CORE_LAST)
    quarter1 = split_back(*half1)
    quarter0 = split_back(*half0)
    conv.step()
    total1 = finish_back(1, back1, *quarter1)
    total0 = finish_back(0, back0, *quarter0)
    conv.finish()
    backward = [None, None]
    backward[1] = spread(pick(order, *total1, 1))

    made1, half1 = feed_back(1, backward[1], True, CORE)
    backward[0] = spread(pick(order, *total0, 1))
    half1 = to_chip(*half1, CHIP)
    made0, half0 = feed_back(0, backward[0], True, CORE)

    def make_feed(refs, q, index):
        result = 0.0
        for i in chunks:
            acts, branch, normed, pre = refs[4 * i : 4 * i + 4]
            left, right = (normed, pre) if q else (acts, branch)
            result = result + t_dot(left[:, block_at(index)], right[...])
        return result

    def place_feed(q, index):
        return [(slice(None), q, (block_at(index),))]

    operands = []
    for i, made in enumerate((made0, made1)):
        operands += [kept_f[i][4], made[4], kept_f[i][3], made[5]]
    feeding = Task(
        ring_sum(
            order, operands, make_feed, width, [(width, width)] * 2, place_feed
        )
    )
    feeding.step()
    half0 = to_chip(*half0, CHIP)
    feeding.step()
    half1 = to_core(*half1, CORE)
    back1 = attend_back(1, made1[0], half1, [], True)
    feeding.step(2)
    half0 = to_core(*half0, CORE)
    back0 = attend_back(0, made0[0], half0, [*back1[4:6], *back1[10:12]], True)
    grads = [back0[4:], back1[6:]]
    memory_grads = grads[0][4:6]

    def make_attend(refs, q, index):
        at = block_at(index)
        memory_ref, memory_grad = refs[0], refs[1 + q]
        one, two = 0.0, t_dot(memory_ref[:, at], memory_grad[...])
        for i in chunks:
            normed, mixed, dq, dk, dv, attend_grad = refs[3 + 6 * i : 9 + 6 * i]
            if q:
                two = two + t_dot(normed[:, at], dv[...])
                one = one + t_dot(mixed[...], attend_grad[:, at])
            else:
                two = two + t_dot(normed[:, at], dk[...])
                one = one + t_dot(normed[:, at], dq[...])
        return jnp.concatenate([one, two], 1)

    def place_attend(q, index):
        at, one, two = block_at(index), slice(0, local), slice(local, 2 * local)
        if q:
            return [(one, 3, (slice(None), at)), (two, 2, (at,))]
        return [(one, 0, (at,)), (two, 1, (at,))]

    operands = [memory_low, *memory_grads]
    for i in chunks:
        operands += [kept_a[i][8], kept_a[i][11], *grads[i][:4]]
    sums_m = memory_sums(order, older, memory, *memory_grads, key_w, value_w)

    def pack(flag, a0, a1, m, f0, f1, cot, out):
        for i in range(2):
            at = slice(i * width // 2, (i + 1) * width // 2)
            start = 8 * i
            out[start : start + 2, :] = a0[0:2, at] + a1[0:2, at] + m[:, at]
            out[start + 2 : start + 4, :] = f0[0:2, at] + f1[0:2, at]
            out[start + 4 : start + 5, :] = a0[2:3, at] + a1[2:3, at]
            out[start + 5 : start + 7, :] = f0[2:4, at] + f1[2:4, at]
            out[start + 7 : start + 8, :] = jnp.zeros_like(out[start + 7 : start + 8, :])
        out[7:8, :local] = jnp.sum(wide(cot[...]), 0, keepdims=True)

    args = [grads[0][6], grads[1][6], sums_m, made0[6], made1[6], squeeze_cot]
    small = order.call(pack, [((16, width // 2), F32)], args)[0]
    attending = Task(
        ring_sum(
            order,
            operands,
            make_attend,
            2 * local,
            [(width, local)] * 3 + [(local, width)],
            place_attend,
            small,
        )
    )

    def small_sums(value):
        total = add(order, value, send(value, CORE))
        yield
        total = add(order, total, send(total, CHIP))
        yield

        def unpack(flag, shared, own, out):
            for i in range(2):
                at = slice(i * width // 2, (i + 1) * width // 2)
                out[0:4, at] = shared[8 * i : 8 * i + 4, :]
                out[4:8, at] = own[8 * i + 4 : 8 * i + 8, :]

        return order.call(unpack, [((8, width), F32)], [total, value])[0]

    def sum_rows(own, other):
        half = add(order, own, send(other, CORE))
        arrived = send(half, CHIP)
        yield
        half = add(order, half, arrived)
        arrived = send(half, CORE)
        yield
        return half, arrived

    def put_chunk(out, i, core, half, twin):
        for at, source in ((core, half), (1 - core, twin)):
            out[at_rows(2 * i + at, HALF), :] = source[i * HALF : (i + 1) * HALF, :]

    def layer_output():
        def kernel(flag, *refs):
            wf, own, other, acc = refs[-4:]
            for i in chunks:
                acc[...] = dot(refs[i][...], wf[...])
                at = slice(i * HALF, (i + 1) * HALF)
                own[at, :] = acc[at_rows(flag[CORE_AT], HALF), :]
                other[at, :] = acc[at_rows(1 - flag[CORE_AT], HALF), :]

        args = [kept[4] for kept in kept_f] + [outer_w]
        outs = [((SEG // 2, width), F32)] * 2
        own, other = order.call(kernel, outs, args, scratch=[pltpu.VMEM((CHUNK, width), F32)])
        yield
        half, twin = yield from sum_rows(own, other)

        def kernel(flag, half_ref, twin_ref, bias, *refs):
            out, acc = refs[-2:]
            for i in chunks:
                hidden, pieces = refs[5 * i], refs[5 * i + 1 : 5 * i + 5]
                put_chunk(out, i, flag[CORE_AT], half_ref, twin_ref)
                put_pieces(acc, pieces, flag[CORE_AT], flag[ON_AT])
                at = chunk_rows(i)
                own_out = out[at, :] + hidden[...] + wide(bias[...])
                out[at, :] = jnp.where(flag[FIRST_AT] == 1, acc[...], own_out)

        args = [half, twin, outer_bias]
        for i in chunks:
            args += [kept_f[i][0], *forward[i]]
        return order.call(
            kernel, [((SEG, width), F32)], args, scratch=[pltpu.VMEM((CHUNK, width), F32)]
        )[0]

    def input_gradient():
        def kernel(flag, a0, b0, c0, a1, b1, c1, own, other):
            own[:HALF, :], own[HALF:, :] = a0[...], a1[...]
            for i, ref in enumerate((b0, c0, b1, c1)):
                other[i * QUARTER : (i + 1) * QUARTER, :] = ref[...]

        outs = [((SEG // 2, width), F32)] * 2
        own, other = order.call(kernel, outs, [*back0[1:4], *back1[1:4]])
        yield
        half, twin = yield from sum_rows(own, other)

        def kernel(flag, half_ref, twin_ref, gain, *refs):
            out, acc = refs[-2:]
            for i in chunks:
                hat, inverse, hidden_grad, *pieces = refs[7 * i : 7 * i + 7]
                put_chunk(out, i, flag[CORE_AT], half_ref, twin_ref)
                put_pieces(acc, pieces, flag[CORE_AT], flag[BACK_AT])
                at = chunk_rows(i)
                grad = standardize_back(out[at, :] * wide(gain[...]), hat[...], inverse[...])
                out[at, :] = jnp.where(flag[FIRST_AT] == 1, hidden_grad[...] + grad, acc[...])

        args = [half, twin, attn_gain]
        for i, back in enumerate((back0, back1)):
            args += [kept_a[i][6], kept_a[i][7], back[0], *backward[i]]
        return order.call(
            kernel, [((SEG, width), F32)], args, scratch=[pltpu.VMEM((CHUNK, width), F32)]
        )[0]

    outward, inward = Task(layer_output()), Task(input_gradient())
    attending.step(2)
    outward.step()
    new_compressed = squeeze(order, memory, older, conv_weight[0], conv_bias)
    attending.step(2)
    outward.step()
    feeding.step(2)
    feeding.step(2)
    attending.step(2)
    feeding.step(2)
    attending.step(2)
    outward.step()
    feeding.step(2)
    attending.step(2)
    outward.finish()
    feeding.step(2)
    attending.step(2)
    inward.step(2)
    attending.step(2)
    inward.step()
    feeding.step(2)
    inward.step()
    attending.step(2)
    small = Task(small_sums(attending.extra))
    small.step()
    inward.finish()
    small.step()
    attending.step()
    small.finish()
    feeding.step()
    outer_g, inner_g = feeding.finish()
    query_g, key_g, value_g, output_g, _ = attending.finish()
    total = small.result
    return (
        outward.result[None],
        new_compressed[None, None],
        inward.result[None],
        query_g[None],
        key_g[None],
        value_g[None],
        output_g[None],
        total[4][None],
        inner_g[None],
        total[6][None],
        outer_g[None],
        total[5][None],
        conv.result[0][None],
        total[7, :local][None],
        total[0][None],
        total[1][None],
        total[2][None],
        total[3][None],
    )


def solution(mesh):
    return jax.shard_map(
        body,
        mesh=mesh,
        in_specs=(
            P("dp", None),
            P("pipe", "dp", None, None),
            P("pipe", "dp", None, None),
            P("dp", None),
            P("dp", None),
            P("pipe", "dp", None, "tensor"),
            P("pipe", None, "tensor"),
            P("pipe", None, "tensor"),
            P("pipe", None, "tensor"),
            P("pipe", "tensor", None),
            P("pipe", None),
            P("pipe", None, "tensor"),
            P("pipe", "tensor"),
            P("pipe", "tensor", None),
            P("pipe", None),
            P("pipe", None, None, "tensor"),
            P("pipe", "tensor"),
            P("pipe", None),
            P("pipe", None),
            P("pipe", None),
            P("pipe", None),
        ),
        out_specs=(
            P("pipe", "dp", None),
            P("pipe", "dp", None, "tensor"),
            P("pipe", "dp", None),
            P("pipe", None, "tensor"),
            P("pipe", None, "tensor"),
            P("pipe", None, "tensor"),
            P("pipe", "tensor", None),
            P("pipe", None),
            P("pipe", None, "tensor"),
            P("pipe", "tensor"),
            P("pipe", "tensor", None),
            P("pipe", None),
            P("pipe", None, None, "tensor"),
            P("pipe", "tensor"),
            P("pipe", None),
            P("pipe", None),
            P("pipe", None),
            P("pipe", None),
        ),
        check_vma=False,
    )
```

time: 680 us -> 477 us (0.70)
  Pallas kernels: 0 us -> 122 us
  other arithmetic: 111 us -> 0 us
  waiting for transfers between devices: 288 us -> 183 us
  matrix products: 74 us -> 0 us
  local copies, waits for them, and re-layouts: 70.5 us -> 7.28 us
  starting transfers between devices: 109 us -> 153 us
  between operations: 17.4 us -> 2.77 us
    pallas_call x0 -> x89, Pallas kernels: none -> 122 us  [call(): pl.pallas_call(kernel, out_shape=[jax.ShapeDtypeStruct(shape, dtype) for...]
    ppermute x98 -> x124, waiting for transfers between devices: 288 us -> 183 us  [send(): return lax.ppermute(value, AXES, moves)]
    dot_general x58 -> x0, matrix products: 74 us -> none  [the longest x21 33.5 us: dot_t(): lax.dot_general(left, right, (((1,), (1,)), ((), ())), preferred_element_...]
    ppermute x98 -> x124, starting transfers between devices: 109 us -> 153 us  [send(): return lax.ppermute(value, AXES, moves)]
    reduce_sum x21 -> x0, other arithmetic: 32.2 us -> none  [the longest x3 6.22 us: standardize_back(): jnp.mean(grad, -1, keepdims=True)]
    add x47 -> x0, other arithmetic: 26.3 us -> none  [the longest x8 8.72 us: chip_sum(): rows(value, core * half, half)]
    unnamed x301 -> x54, local copies, waits for them, and re-layouts: 29.6 us -> 6.01 us
    concatenate x24 -> x0, other arithmetic: 21.6 us -> none  [the longest x6 15.4 us: ring_sum(): return jnp.roll(total, (here, there), (0, 1)).reshape(shape)]
  transfers between devices with their start and end apart: 99 -> 124, of which waited for: 44 -> 52; matrix products, arithmetic and copies ran while one was open for 19% -> 0% of each run, Pallas kernels for 0% -> 21%
where the time goes in v2:
time: 477 us; the launch traced here: 468 us
  waiting for transfers between devices  183 us (38%)
  starting transfers between devices  153 us (32%)
  Pallas kernels  122 us (26%)
  local copies, waits for them, and re-layouts  7.28 us (2%)
    ppermute x124, waiting for transfers between devices, send(): return lax.ppermute(value, AXES, moves)  183 us
    ppermute x124, starting transfers between devices, send(): return lax.ppermute(value, AXES, moves)  153 us
    pallas_call x89, Pallas kernels, call(): pl.pallas_call(kernel, out_shape=[jax.ShapeDtypeStruct(shape, dtype) for...  122 us
  transfers between devices with their start and end apart: 124, of which 52 were waited for; matrix products, arithmetic and copies ran while one was open for 0% of the time, Pallas kernels for 21%

profile of v2, /device:TPU:0, one launch (start us, length us, event | category | flops | bytes accessed | tf_op | source)
XLA Modules:
  0.0 467.8 jit_solution(10871792175308285846)
XLA Ops:
  6.7 3.7 shard_map.340
  10.5 3.0 shard_map.341
  17.9 3.4 shard_map.342
  26.4 3.5 collective-permute-start.6
  35.1 4.3 collective-permute-done.4.refs_2_
  47.1 3.5 collective-permute-start.11
  52.5 2.6 shard_map.348
  65.6 3.1 collective-permute-start.15
  73.8 2.6 shard_map.353
  95.3 6.6 %collective-permute-done.25.refs_3_.refs_2_ = f32[64,1024]{1,0:T(8,128)S(1)} collective-permute-done((f32[64,1024]{1,0:T(8,128)S(1)}, f32[64,1024]{1,0:T(8,128)S(1)}, u32[]{:S(2)}, u32[]{:S(2)}) %collective-permute-start.25) | collective-permute-done | bytes 262176 | tf_op jit(solution)/shard_map/ppermute | solution.py:68
  102.0 4.3 collective-permute-start.28
  109.6 2.9 collective-permute-done.23.below_ref
  113.2 3.1 shard_map.359
  117.8 6.8 %collective-permute-done.31.refs_3_.refs_7_ = f32[64,1024]{1,0:T(8,128)S(1)} collective-permute-done((f32[64,1024]{1,0:T(8,128)S(1)}, f32[64,1024]{1,0:T(8,128)S(1)}, u32[]{:S(2)}, u32[]{:S(2)}) %collective-permute-start.31) | collective-permute-done | bytes 262176 | tf_op jit(solution)/shard_map/ppermute | solution.py:68
  126.5 3.2 shard_map.362
  131.0 2.6 collective-permute-start.37
  152.5 6.0 %collective-permute-done.45.b = f32[128,1024]{1,0:T(8,128)S(1)} collective-permute-done((f32[128,1024]{1,0:T(8,128)S(1)}, f32[128,1024]{1,0:T(8,128)S(1)}, u32[]{:S(2)}, u32[]{:S(2)}) %collective-permute-start.45) | collective-permute-done | bytes 524320 | tf_op jit(solution)/shard_map/ppermute | solution.py:68
  172.3 5.1 %collective-permute-done.50.below_ref = f32[512,256]{1,0:T(8,128)S(1)} collective-permute-done((f32[512,256]{1,0:T(8,128)S(1)}, f32[512,256]{1,0:T(8,128)S(1)}, u32[]{:S(2)}, u32[]{:S(2)}) %collective-permute-start.50) | collective-permute-done | bytes 524320 | tf_op jit(solution)/shard_map/ppermute | solution.py:68
  182.1 4.3 shard_map.377
  187.8 3.8 shard_map.378
  195.4 2.5 collective-permute-start.65
  205.0 41.3 %collective-permute-done.66.a = f32[64,1024]{1,0:T(8,128)S(1)} collective-permute-done((f32[64,1024]{1,0:T(8,128)S(1)}, f32[64,1024]{1,0:T(8,128)S(1)}, u32[]{:S(2)}, u32[]{:S(2)}) %collective-permute-start.66) | collective-permute-done | bytes 262176 | tf_op jit(solution)/shard_map/ppermute | solution.py:68
  247.6 5.8 %collective-permute-done.67.refs_3_.refs_11_ = f32[64,1024]{1,0:T(8,128)S(1)} collective-permute-done((f32[64,1024]{1,0:T(8,128)S(1)}, f32[64,1024]{1,0:T(8,128)S(1)}, u32[]{:S(2)}, u32[]{:S(2)}) %collective-permute-start.67) | collective-permute-done | bytes 262176 | tf_op jit(solution)/shard_map/ppermute | solution.py:68
  257.3 8.0 %collective-permute-done.70.a = f32[64,1024]{1,0:T(8,128)S(1)} collective-permute-done((f32[64,1024]{1,0:T(8,128)S(1)}, f32[64,1024]{1,0:T(8,128)S(1)}, u32[]{:S(2)}, u32[]{:S(2)}) %collective-permute-start.70) | collective-permute-done | bytes 262176 | tf_op jit(solution)/shard_map/ppermute | solution.py:68
  266.6 7.2 %collective-permute-done.73.refs_3_.refs_4_ = f32[64,1024]{1,0:T(8,128)S(1)} collective-permute-done((f32[64,1024]{1,0:T(8,128)S(1)}, f32[64,1024]{1,0:T(8,128)S(1)}, u32[]{:S(2)}, u32[]{:S(2)}) %collective-permute-start.73) | collective-permute-done | bytes 262176 | tf_op jit(solution)/shard_map/ppermute | solution.py:68
  280.3 2.8 collective-permute-start.81
  284.1 12.9 %collective-permute-done.78.b = f32[128,1024]{1,0:T(8,128)S(1)} collective-permute-done((f32[128,1024]{1,0:T(8,128)S(1)}, f32[128,1024]{1,0:T(8,128)S(1)}, u32[]{:S(2)}, u32[]{:S(2)}) %collective-permute-start.78) | collective-permute-done | bytes 524320 | tf_op jit(solution)/shard_map/ppermute | solution.py:68
  299.6 4.7 %shard_map.393 = (f32[256,1024]{1,0:T(8,128)S(1)}, f32[128,1024]{1,0:T(8,128)S(1)}, f32[64,1024]{1,0:T(8,128)S(1)}, f32[64,1024]{1,0:T(8,128)S(1)}, f32[256,256]...) custom-call(s32[7]{0:T(128)S(1)} %stack.31.flag.refs_0_, ...), custom_call_target="tpu_custom_call" | custom-call | flops 1 | bytes 1 | tf_op jit(solution)/shard_map/pallas_call | solution.py:133
  306.2 2.8 collective-permute-start.89
  309.7 2.8 collective-permute-done.83.b
  315.1 4.4 shard_map.396
  326.2 2.7 collective-permute-start.86
  332.0 7.6 %collective-permute-done.86.refs_16_ = f32[272,512]{1,0:T(8,128)S(1)} collective-permute-done((f32[272,512]{1,0:T(8,128)S(1)}, f32[272,512]{1,0:T(8,128)S(1)}, u32[]{:S(2)}, u32[]{:S(2)}) %collective-permute-start.86) | collective-permute-done | bytes 557088 | tf_op jit(solution)/shard_map/ppermute | solution.py:68
  349.7 3.2 collective-permute-start.92
  352.9 6.1 %collective-permute-done.91.below_ref = f32[64,1024]{1,0:T(8,128)S(1)} collective-permute-done((f32[64,1024]{1,0:T(8,128)S(1)}, f32[64,1024]{1,0:T(8,128)S(1)}, u32[]{:S(2)}, u32[]{:S(2)}) %collective-permute-start.91) | collective-permute-done | bytes 262176 | tf_op jit(solution)/shard_map/ppermute | solution.py:68
  359.7 3.2 collective-permute-start.96
  364.6 3.2 collective-permute-start.98
  376.7 3.2 collective-permute-start.103
  379.8 3.8 collective-permute-done.100.below_ref
  391.5 2.7 collective-permute-start.108
  394.1 2.7 shard_map.412
  408.0 4.4 collective-permute-done.110.far_p_ref
  413.3 15.7 %collective-permute-done.112.refs_1_ = f32[256,1024]{1,0:T(8,128)S(1)} collective-permute-done((f32[256,1024]{1,0:T(8,128)S(1)}, f32[256,1024]{1,0:T(8,128)S(1)}, u32[]{:S(2)}, u32[]{:S(2)}) %collective-permute-start.112) | collective-permute-done | bytes 1048608 | tf_op jit(solution)/shard_map/ppermute | solution.py:68
  434.3 3.1 collective-permute-start.121
  437.4 3.2 shard_map.420
  440.6 5.6 %collective-permute-done.116.below_ref = f32[512,512]{1,0:T(8,128)S(1)} collective-permute-done((f32[512,512]{1,0:T(8,128)S(1)}, f32[512,512]{1,0:T(8,128)S(1)}, u32[]{:S(2)}, u32[]{:S(2)}) %collective-permute-start.116) | collective-permute-done | bytes 1048608 | tf_op jit(solution)/shard_map/ppermute | solution.py:68
  453.1 2.9 collective-permute-done.119.refs_1_
  459.4 3.3 shard_map.426
  (346 shorter events, 214.7 us)
Async XLA Ops:
  13.5 12.3 %collective-permute-start = (f32[64,1024]{1,0:T(8,128)S(1)}, f32[64,1024]{1,0:T(8,128)S(1)}, u32[]{:S(2)}, u32[]{:S(2)}) collective-permute-start(f32[64,1024]{1,0:T(8,128)S(1)} %get-tuple-element.373), channel_id=1, source_target_pairs={{0,1},{1,0},{2,3},{3,2},{4,5},{5,4},{6,7},{7,6},{8,9},{9,8},{10,11... | collective-permute-start | bytes 786440 | tf_op jit(solution)/shard_map/ppermute | solution.py:68
  15.5 10.3 %collective-permute-start.1 = (f32[64,1024]{1,0:T(8,128)S(1)}, f32[64,1024]{1,0:T(8,128)S(1)}, u32[]{:S(2)}, u32[]{:S(2)}) collective-permute-start(f32[64,1024]{1,0:T(8,128)S(1)} %get-tuple-element.374), channel_id=1, source_target_pairs={{0,1},{1,0},{2,3},{3,2},{4,5},{5,4},{6,7},{7,6},{8,9},{9,8},{10,11... | collective-permute-start | bytes 786440 | tf_op jit(solution)/shard_map/ppermute | solution.py:68
  26.4 15.7 %collective-permute-start.6 = (f32[128,1024]{1,0:T(8,128)S(1)}, f32[128,1024]{1,0:T(8,128)S(1)}, u32[]{:S(2)}, u32[]{:S(2)}) collective-permute-start(f32[128,1024]{1,0:T(8,128)S(1)} %shard_map.343.a), channel_id=1, source_target_pairs={{0,2},{1,3},{2,0},{3,1},{4,6},{5,7},{6,4},{7,5},{8,10},{9,11},{10,... | collective-permute-start | bytes 1572872 | tf_op jit(solution)/shard_map/ppermute | solution.py:68
  42.8 9.7 %collective-permute-start.7 = (f32[64,1024]{1,0:T(8,128)S(1)}, f32[64,1024]{1,0:T(8,128)S(1)}, u32[]{:S(2)}, u32[]{:S(2)}) collective-permute-start(f32[64,1024]{1,0:T(8,128)S(1)} %get-tuple-element.389), channel_id=1, source_target_pairs={{0,1},{1,0},{2,3},{3,2},{4,5},{5,4},{6,7},{7,6},{8,9},{9,8},{10,11... | collective-permute-start | bytes 786440 | tf_op jit(solution)/shard_map/ppermute | solution.py:68
  47.1 17.9 %collective-permute-start.11 = (f32[128,1024]{1,0:T(8,128)S(1)}, f32[128,1024]{1,0:T(8,128)S(1)}, u32[]{:S(2)}, u32[]{:S(2)}) collective-permute-start(f32[128,1024]{1,0:T(8,128)S(1)} %shard_map.344.a), channel_id=1, source_target_pairs={{0,2},{1,3},{2,0},{3,1},{4,6},{5,7},{6,4},{7,5},{8,10},{9,11},{10,... | collective-permute-start | bytes 1572872 | tf_op jit(solution)/shard_map/ppermute | solution.py:68
  50.6 20.0 %collective-permute-start.12 = (f32[512,256]{1,0:T(8,128)S(1)}, f32[512,256]{1,0:T(8,128)S(1)}, u32[]{:S(2)}, u32[]{:S(2)}) collective-permute-start(f32[512,256]{1,0:T(8,128)S(1)} %get-tuple-element.401), channel_id=1, source_target_pairs={{0,16},{1,5},{2,18},{3,7},{4,20},{5,9},{6,22},{7,11},{8,24},{9,13}... | collective-permute-start | bytes 1572872 | tf_op jit(solution)/shard_map/ppermute | solution.py:68
  59.5 11.2 %collective-permute-start.13 = (f32[512,256]{1,0:T(8,128)S(1)}, f32[512,256]{1,0:T(8,128)S(1)}, u32[]{:S(2)}, u32[]{:S(2)}) collective-permute-start(f32[512,256]{1,0:T(8,128)S(1)} %get-tuple-element.402), channel_id=1, source_target_pairs={{0,48},{1,13},{2,50},{3,15},{4,52},{5,1},{6,54},{7,3},{8,56},{9,5}... | collective-permute-start | bytes 1572872 | tf_op jit(solution)/shard_map/ppermute | solution.py:68
  62.5 10.7 %collective-permute-start.14 = (f32[64,1024]{1,0:T(8,128)S(1)}, f32[64,1024]{1,0:T(8,128)S(1)}, u32[]{:S(2)}, u32[]{:S(2)}) collective-permute-start(f32[64,1024]{1,0:T(8,128)S(1)} %get-tuple-element.405), channel_id=1, source_target_pairs={{0,2},{1,3},{2,0},{3,1},{4,6},{5,7},{6,4},{7,5},{8,10},{9,11},{10,... | collective-permute-start | bytes 786440 | tf_op jit(solution)/shard_map/ppermute | solution.py:68
  82.7 10.4 %collective-permute-start.21 = (f32[64,1024]{1,0:T(8,128)S(1)}, f32[64,1024]{1,0:T(8,128)S(1)}, u32[]{:S(2)}, u32[]{:S(2)}) collective-permute-start(f32[64,1024]{1,0:T(8,128)S(1)} %get-tuple-element.423), channel_id=1, source_target_pairs={{0,2},{1,3},{2,0},{3,1},{4,6},{5,7},{6,4},{7,5},{8,10},{9,11},{10,... | collective-permute-start | bytes 786440 | tf_op jit(solution)/shard_map/ppermute | solution.py:68
  95.3 17.8 %collective-permute-start.26 = (f32[64,1024]{1,0:T(8,128)S(1)}, f32[64,1024]{1,0:T(8,128)S(1)}, u32[]{:S(2)}, u32[]{:S(2)}) collective-permute-start(f32[64,1024]{1,0:T(8,128)S(1)} %shard_map.357.refs_2_.refs_1_), channel_id=1, source_target_pairs={{0,1},{1,0},{2,3},{3,2},{4,5},{5,4},{6,7},{7,6},{8,9},{9,8},{10,11... | collective-permute-start | bytes 786440 | tf_op jit(solution)/shard_map/ppermute | solution.py:68
  102.0 11.2 %collective-permute-start.27 = (f32[64,1024]{1,0:T(8,128)S(1)}, f32[64,1024]{1,0:T(8,128)S(1)}, u32[]{:S(2)}, u32[]{:S(2)}) collective-permute-start(f32[64,1024]{1,0:T(8,128)S(1)} %collective-permute-done.25.refs_3_.refs_2_), channel_id=1, source_target_pairs={{0,1},{1,0},{2,3},{3,2},{4,5},{5,4},{6,7},{7,6},{8,9},{9,8},{10,11... | collective-permute-start | bytes 786440 | tf_op jit(solution)/shard_map/ppermute | solution.py:68
  102.0 14.4 %collective-permute-start.28 = (f32[64,1024]{1,0:T(8,128)S(1)}, f32[64,1024]{1,0:T(8,128)S(1)}, u32[]{:S(2)}, u32[]{:S(2)}) collective-permute-start(f32[64,1024]{1,0:T(8,128)S(1)} %shard_map.356.b), channel_id=1, source_target_pairs={{0,66},{1,67},{2,64},{3,65},{4,70},{5,71},{6,68},{7,69},{8,74},{9,... | collective-permute-start | bytes 786440 | tf_op jit(solution)/shard_map/ppermute | solution.py:68
  125.6 17.8 %collective-permute-start.40 = (f32[128,1024]{1,0:T(8,128)S(1)}, f32[128,1024]{1,0:T(8,128)S(1)}, u32[]{:S(2)}, u32[]{:S(2)}) collective-permute-start(f32[128,1024]{1,0:T(8,128)S(1)} %shard_map.361.a), channel_id=1, source_target_pairs={{0,2},{1,3},{2,0},{3,1},{4,6},{5,7},{6,4},{7,5},{8,10},{9,11},{10,... | collective-permute-start | bytes 1572872 | tf_op jit(solution)/shard_map/ppermute | solution.py:68
  144.6 13.9 %collective-permute-start.45 = (f32[128,1024]{1,0:T(8,128)S(1)}, f32[128,1024]{1,0:T(8,128)S(1)}, u32[]{:S(2)}, u32[]{:S(2)}) collective-permute-start(f32[128,1024]{1,0:T(8,128)S(1)} %shard_map.363.a), channel_id=1, source_target_pairs={{0,2},{1,3},{2,0},{3,1},{4,6},{5,7},{6,4},{7,5},{8,10},{9,11},{10,... | collective-permute-start | bytes 1572872 | tf_op jit(solution)/shard_map/ppermute | solution.py:68
  167.0 10.5 %collective-permute-start.50 = (f32[512,256]{1,0:T(8,128)S(1)}, f32[512,256]{1,0:T(8,128)S(1)}, u32[]{:S(2)}, u32[]{:S(2)}) collective-permute-start(f32[512,256]{1,0:T(8,128)S(1)} %shard_map.365.own_ref), channel_id=1, source_target_pairs={{0,16},{1,5},{2,18},{3,7},{4,20},{5,9},{6,22},{7,11},{8,24},{9,13}... | collective-permute-start | bytes 1572872 | tf_op jit(solution)/shard_map/ppermute | solution.py:68
  194.3 9.4 %collective-permute-start.64 = (f32[256,256]{1,0:T(8,128)S(1)}, f32[256,256]{1,0:T(8,128)S(1)}, u32[]{:S(2)}, u32[]{:S(2)}) collective-permute-start(f32[256,256]{1,0:T(8,128)S(1)} %get-tuple-element.528), channel_id=1, source_target_pairs={{0,16},{1,5},{2,18},{3,7},{4,20},{5,9},{6,22},{7,11},{8,24},{9,13}... | collective-permute-start | bytes 786440 | tf_op jit(solution)/shard_map/ppermute | solution.py:68
  201.6 44.7 %collective-permute-start.66 = (f32[64,1024]{1,0:T(8,128)S(1)}, f32[64,1024]{1,0:T(8,128)S(1)}, u32[]{:S(2)}, u32[]{:S(2)}) collective-permute-start(f32[64,1024]{1,0:T(8,128)S(1)} %shard_map.382.b), channel_id=1, source_target_pairs={{64,2},{65,3},{66,0},{67,1},{68,6},{69,7},{70,4},{71,5},{72,10},{7... | collective-permute-start | bytes 786440 | tf_op jit(solution)/shard_map/ppermute | solution.py:68
  253.5 11.8 %collective-permute-start.70 = (f32[64,1024]{1,0:T(8,128)S(1)}, f32[64,1024]{1,0:T(8,128)S(1)}, u32[]{:S(2)}, u32[]{:S(2)}) collective-permute-start(f32[64,1024]{1,0:T(8,128)S(1)} %shard_map.383.b), channel_id=1, source_target_pairs={{64,2},{65,3},{66,0},{67,1},{68,6},{69,7},{70,4},{71,5},{72,10},{7... | collective-permute-start | bytes 786440 | tf_op jit(solution)/shard_map/ppermute | solution.py:68
  280.3 24.0 %collective-permute-start.81 = (f32[256,1024]{1,0:T(8,128)S(1)}, f32[256,1024]{1,0:T(8,128)S(1)}, u32[]{:S(2)}, u32[]{:S(2)}) collective-permute-start(f32[256,1024]{1,0:T(8,128)S(1)} %get-tuple-element.562), channel_id=1, source_target_pairs={{0,16},{1,5},{2,18},{3,7},{4,20},{5,9},{6,22},{7,11},{8,24},{9,13}... | collective-permute-start | bytes 3145736 | tf_op jit(solution)/shard_map/ppermute | solution.py:68
  283.0 21.2 %collective-permute-start.82 = (f32[256,1024]{1,0:T(8,128)S(1)}, f32[256,1024]{1,0:T(8,128)S(1)}, u32[]{:S(2)}, u32[]{:S(2)}) collective-permute-start(f32[256,1024]{1,0:T(8,128)S(1)} %get-tuple-element.563), channel_id=1, source_target_pairs={{0,48},{1,13},{2,50},{3,15},{4,52},{5,1},{6,54},{7,3},{8,56},{9,5}... | collective-permute-start | bytes 3145736 | tf_op jit(solution)/shard_map/ppermute | solution.py:68
  283.8 13.1 %collective-permute-start.78 = (f32[128,1024]{1,0:T(8,128)S(1)}, f32[128,1024]{1,0:T(8,128)S(1)}, u32[]{:S(2)}, u32[]{:S(2)}) collective-permute-start(f32[128,1024]{1,0:T(8,128)S(1)} %shard_map.388.a), channel_id=1, source_target_pairs={{0,2},{1,3},{2,0},{3,1},{4,6},{5,7},{6,4},{7,5},{8,10},{9,11},{10,... | collective-permute-start | bytes 1572872 | tf_op jit(solution)/shard_map/ppermute | solution.py:68
  298.2 14.3 %collective-permute-start.83 = (f32[128,1024]{1,0:T(8,128)S(1)}, f32[128,1024]{1,0:T(8,128)S(1)}, u32[]{:S(2)}, u32[]{:S(2)}) collective-permute-start(f32[128,1024]{1,0:T(8,128)S(1)} %shard_map.391.a), channel_id=1, source_target_pairs={{0,2},{1,3},{2,0},{3,1},{4,6},{5,7},{6,4},{7,5},{8,10},{9,11},{10,... | collective-permute-start | bytes 1572872 | tf_op jit(solution)/shard_map/ppermute | solution.py:68
  306.2 42.0 %collective-permute-start.89 = (f32[512,1024]{1,0:T(8,128)S(1)}, f32[512,1024]{1,0:T(8,128)S(1)}, u32[]{:S(2)}, u32[]{:S(2)}) collective-permute-start(f32[512,1024]{1,0:T(8,128)S(1)} %get-tuple-element.609), channel_id=1, source_target_pairs={{0,16},{1,5},{2,18},{3,7},{4,20},{5,9},{6,22},{7,11},{8,24},{9,13}... | collective-permute-start | bytes 6291464 | tf_op jit(solution)/shard_map/ppermute | solution.py:68
  308.9 39.2 %collective-permute-start.90 = (f32[512,1024]{1,0:T(8,128)S(1)}, f32[512,1024]{1,0:T(8,128)S(1)}, u32[]{:S(2)}, u32[]{:S(2)}) collective-permute-start(f32[512,1024]{1,0:T(8,128)S(1)} %get-tuple-element.610), channel_id=1, source_target_pairs={{0,48},{1,13},{2,50},{3,15},{4,52},{5,1},{6,54},{7,3},{8,56},{9,5}... | collective-permute-start | bytes 6291464 | tf_op jit(solution)/shard_map/ppermute | solution.py:68
  325.8 20.4 %collective-permute-start.88 = (f32[256,1024]{1,0:T(8,128)S(1)}, f32[256,1024]{1,0:T(8,128)S(1)}, u32[]{:S(2)}, u32[]{:S(2)}) collective-permute-start(f32[256,1024]{1,0:T(8,128)S(1)} %get-tuple-element.606), channel_id=1, source_target_pairs={{0,1},{1,0},{2,3},{3,2},{4,5},{5,4},{6,7},{7,6},{8,9},{9,8},{10,11... | collective-permute-start | bytes 3145736 | tf_op jit(solution)/shard_map/ppermute | solution.py:68
  326.2 13.4 %collective-permute-start.86 = (f32[272,512]{1,0:T(8,128)S(1)}, f32[272,512]{1,0:T(8,128)S(1)}, u32[]{:S(2)}, u32[]{:S(2)}) collective-permute-start(f32[272,512]{1,0:T(8,128)S(1)} %get-tuple-element.602), channel_id=1, source_target_pairs={{0,16},{1,5},{2,18},{3,7},{4,20},{5,9},{6,22},{7,11},{8,24},{9,13}... | collective-permute-start | bytes 1671176 | tf_op jit(solution)/shard_map/ppermute | solution.py:68
  328.9 12.0 %collective-permute-start.87 = (f32[272,512]{1,0:T(8,128)S(1)}, f32[272,512]{1,0:T(8,128)S(1)}, u32[]{:S(2)}, u32[]{:S(2)}) collective-permute-start(f32[272,512]{1,0:T(8,128)S(1)} %get-tuple-element.603), channel_id=1, source_target_pairs={{0,48},{1,13},{2,50},{3,15},{4,52},{5,1},{6,54},{7,3},{8,56},{9,5}... | collective-permute-start | bytes 1671176 | tf_op jit(solution)/shard_map/ppermute | solution.py:68
  342.9 20.0 %collective-permute-start.93 = (f32[528,512]{1,0:T(8,128)S(1)}, f32[528,512]{1,0:T(8,128)S(1)}, u32[]{:S(2)}, u32[]{:S(2)}) collective-permute-start(f32[528,512]{1,0:T(8,128)S(1)} %get-tuple-element.621), channel_id=1, source_target_pairs={{0,16},{1,5},{2,18},{3,7},{4,20},{5,9},{6,22},{7,11},{8,24},{9,13}... | collective-permute-start | bytes 3244040 | tf_op jit(solution)/shard_map/ppermute | solution.py:68
  344.2 18.9 %collective-permute-start.94 = (f32[528,512]{1,0:T(8,128)S(1)}, f32[528,512]{1,0:T(8,128)S(1)}, u32[]{:S(2)}, u32[]{:S(2)}) collective-permute-start(f32[528,512]{1,0:T(8,128)S(1)} %get-tuple-element.622.refs_15_), channel_id=1, source_target_pairs={{0,48},{1,13},{2,50},{3,15},{4,52},{5,1},{6,54},{7,3},{8,56},{9,5}... | collective-permute-start | bytes 3244040 | tf_op jit(solution)/shard_map/ppermute | solution.py:68
  346.9 25.6 %collective-permute-start.99 = (f32[256,1024]{1,0:T(8,128)S(1)}, f32[256,1024]{1,0:T(8,128)S(1)}, u32[]{:S(2)}, u32[]{:S(2)}) collective-permute-start(f32[256,1024]{1,0:T(8,128)S(1)} %shard_map.403.refs_0_), channel_id=1, source_target_pairs={{0,2},{1,3},{2,0},{3,1},{4,6},{5,7},{6,4},{7,5},{8,10},{9,11},{10,... | collective-permute-start | bytes 3145736 | tf_op jit(solution)/shard_map/ppermute | solution.py:68
  349.6 9.4 %collective-permute-start.91 = (f32[64,1024]{1,0:T(8,128)S(1)}, f32[64,1024]{1,0:T(8,128)S(1)}, u32[]{:S(2)}, u32[]{:S(2)}) collective-permute-start(f32[64,1024]{1,0:T(8,128)S(1)} %get-tuple-element.616), channel_id=1, source_target_pairs={{0,4},{1,17},{2,6},{3,19},{4,8},{5,21},{6,10},{7,23},{8,12},{9,25}... | collective-permute-start | bytes 786440 | tf_op jit(solution)/shard_map/ppermute | solution.py:68
  349.7 9.3 %collective-permute-start.92 = (f32[64,1024]{1,0:T(8,128)S(1)}, f32[64,1024]{1,0:T(8,128)S(1)}, u32[]{:S(2)}, u32[]{:S(2)}) collective-permute-start(f32[64,1024]{1,0:T(8,128)S(1)} %get-tuple-element.617), channel_id=1, source_target_pairs={{0,12},{1,49},{2,14},{3,51},{4,0},{5,53},{6,2},{7,55},{8,4},{9,57}... | collective-permute-start | bytes 786440 | tf_op jit(solution)/shard_map/ppermute | solution.py:68
  359.6 10.5 %collective-permute-start.95 = (f32[128,1024]{1,0:T(8,128)S(1)}, f32[128,1024]{1,0:T(8,128)S(1)}, u32[]{:S(2)}, u32[]{:S(2)}) collective-permute-start(f32[128,1024]{1,0:T(8,128)S(1)} %get-tuple-element.627), channel_id=1, source_target_pairs={{0,4},{1,17},{2,6},{3,19},{4,8},{5,21},{6,10},{7,23},{8,12},{9,25}... | collective-permute-start | bytes 1572872 | tf_op jit(solution)/shard_map/ppermute | solution.py:68
  359.7 10.4 %collective-permute-start.96 = (f32[128,1024]{1,0:T(8,128)S(1)}, f32[128,1024]{1,0:T(8,128)S(1)}, u32[]{:S(2)}, u32[]{:S(2)}) collective-permute-start(f32[128,1024]{1,0:T(8,128)S(1)} %get-tuple-element.628.down_ref), channel_id=1, source_target_pairs={{0,12},{1,49},{2,14},{3,51},{4,0},{5,53},{6,2},{7,55},{8,4},{9,57}... | collective-permute-start | bytes 1572872 | tf_op jit(solution)/shard_map/ppermute | solution.py:68
  373.1 21.0 %collective-permute-start.104 = (f32[256,1024]{1,0:T(8,128)S(1)}, f32[256,1024]{1,0:T(8,128)S(1)}, u32[]{:S(2)}, u32[]{:S(2)}) collective-permute-start(f32[256,1024]{1,0:T(8,128)S(1)} %shard_map.409.half_ref), channel_id=1, source_target_pairs={{0,1},{1,0},{2,3},{3,2},{4,5},{5,4},{6,7},{7,6},{8,9},{9,8},{10,11... | collective-permute-start | bytes 3145736 | tf_op jit(solution)/shard_map/ppermute | solution.py:68
  373.2 10.5 %collective-permute-start.100 = (f32[128,1024]{1,0:T(8,128)S(1)}, f32[128,1024]{1,0:T(8,128)S(1)}, u32[]{:S(2)}, u32[]{:S(2)}) collective-permute-start(f32[128,1024]{1,0:T(8,128)S(1)} %shard_map.407.own_ref), channel_id=1, source_target_pairs={{0,4},{1,17},{2,6},{3,19},{4,8},{5,21},{6,10},{7,23},{8,12},{9,25}... | collective-permute-start | bytes 1572872 | tf_op jit(solution)/shard_map/ppermute | solution.py:68
  376.6 10.2 %collective-permute-start.102 = (f32[144,512]{1,0:T(8,128)S(1)}, f32[144,512]{1,0:T(8,128)S(1)}, u32[]{:S(2)}, u32[]{:S(2)}) collective-permute-start(f32[144,512]{1,0:T(8,128)S(1)} %get-tuple-element.644), channel_id=1, source_target_pairs={{0,4},{1,17},{2,6},{3,19},{4,8},{5,21},{6,10},{7,23},{8,12},{9,25}... | collective-permute-start | bytes 884744 | tf_op jit(solution)/shard_map/ppermute | solution.py:68
  376.7 10.3 %collective-permute-start.103 = (f32[144,512]{1,0:T(8,128)S(1)}, f32[144,512]{1,0:T(8,128)S(1)}, u32[]{:S(2)}, u32[]{:S(2)}) collective-permute-start(f32[144,512]{1,0:T(8,128)S(1)} %get-tuple-element.645.down_ref), channel_id=1, source_target_pairs={{0,12},{1,49},{2,14},{3,51},{4,0},{5,53},{6,2},{7,55},{8,4},{9,57}... | collective-permute-start | bytes 884744 | tf_op jit(solution)/shard_map/ppermute | solution.py:68
  387.6 9.2 %collective-permute-start.105 = (f32[64,1024]{1,0:T(8,128)S(1)}, f32[64,1024]{1,0:T(8,128)S(1)}, u32[]{:S(2)}, u32[]{:S(2)}) collective-permute-start(f32[64,1024]{1,0:T(8,128)S(1)} %get-tuple-element.650), channel_id=1, source_target_pairs={{0,4},{1,17},{2,6},{3,19},{4,8},{5,21},{6,10},{7,23},{8,12},{9,25}... | collective-permute-start | bytes 786440 | tf_op jit(solution)/shard_map/ppermute | solution.py:68
  400.0 33.4 %collective-permute-start.113 = (f32[512,1024]{1,0:T(8,128)S(1)}, f32[512,1024]{1,0:T(8,128)S(1)}, u32[]{:S(2)}, u32[]{:S(2)}) collective-permute-start(f32[512,1024]{1,0:T(8,128)S(1)} %shard_map.413.own_ref), channel_id=1, source_target_pairs={{0,16},{1,5},{2,18},{3,7},{4,20},{5,9},{6,22},{7,11},{8,24},{9,13}... | collective-permute-start | bytes 6291464 | tf_op jit(solution)/shard_map/ppermute | solution.py:68
  401.5 31.9 %collective-permute-start.114 = (f32[512,1024]{1,0:T(8,128)S(1)}, f32[512,1024]{1,0:T(8,128)S(1)}, u32[]{:S(2)}, u32[]{:S(2)}) collective-permute-start(f32[512,1024]{1,0:T(8,128)S(1)} %shard_map.413.own_ref), channel_id=1, source_target_pairs={{0,48},{1,13},{2,50},{3,15},{4,52},{5,1},{6,54},{7,3},{8,56},{9,5}... | collective-permute-start | bytes 6291464 | tf_op jit(solution)/shard_map/ppermute | solution.py:68
  403.9 25.1 %collective-permute-start.112 = (f32[256,1024]{1,0:T(8,128)S(1)}, f32[256,1024]{1,0:T(8,128)S(1)}, u32[]{:S(2)}, u32[]{:S(2)}) collective-permute-start(f32[256,1024]{1,0:T(8,128)S(1)} %shard_map.416.refs_0_), channel_id=1, source_target_pairs={{0,2},{1,3},{2,0},{3,1},{4,6},{5,7},{6,4},{7,5},{8,10},{9,11},{10,... | collective-permute-start | bytes 3145736 | tf_op jit(solution)/shard_map/ppermute | solution.py:68
  429.9 16.3 %collective-permute-start.116 = (f32[512,512]{1,0:T(8,128)S(1)}, f32[512,512]{1,0:T(8,128)S(1)}, u32[]{:S(2)}, u32[]{:S(2)}) collective-permute-start(f32[512,512]{1,0:T(8,128)S(1)} %shard_map.417.own_ref), channel_id=1, source_target_pairs={{0,16},{1,5},{2,18},{3,7},{4,20},{5,9},{6,22},{7,11},{8,24},{9,13}... | collective-permute-start | bytes 3145736 | tf_op jit(solution)/shard_map/ppermute | solution.py:68
  431.5 14.8 %collective-permute-start.117 = (f32[512,512]{1,0:T(8,128)S(1)}, f32[512,512]{1,0:T(8,128)S(1)}, u32[]{:S(2)}, u32[]{:S(2)}) collective-permute-start(f32[512,512]{1,0:T(8,128)S(1)} %shard_map.417.own_ref), channel_id=1, source_target_pairs={{0,48},{1,13},{2,50},{3,15},{4,52},{5,1},{6,54},{7,3},{8,56},{9,5}... | collective-permute-start | bytes 3145736 | tf_op jit(solution)/shard_map/ppermute | solution.py:68
  434.1 28.6 %collective-permute-start.120 = (f32[256,1024]{1,0:T(8,128)S(1)}, f32[256,1024]{1,0:T(8,128)S(1)}, u32[]{:S(2)}, u32[]{:S(2)}) collective-permute-start(f32[256,1024]{1,0:T(8,128)S(1)} %get-tuple-element.690), channel_id=1, source_target_pairs={{0,16},{1,5},{2,18},{3,7},{4,20},{5,9},{6,22},{7,11},{8,24},{9,13}... | collective-permute-start | bytes 3145736 | tf_op jit(solution)/shard_map/ppermute | solution.py:68
  434.3 28.4 %collective-permute-start.121 = (f32[256,1024]{1,0:T(8,128)S(1)}, f32[256,1024]{1,0:T(8,128)S(1)}, u32[]{:S(2)}, u32[]{:S(2)}) collective-permute-start(f32[256,1024]{1,0:T(8,128)S(1)} %get-tuple-element.691), channel_id=1, source_target_pairs={{0,48},{1,13},{2,50},{3,15},{4,52},{5,1},{6,54},{7,3},{8,56},{9,5}... | collective-permute-start | bytes 3145736 | tf_op jit(solution)/shard_map/ppermute | solution.py:68
  447.0 18.9 %collective-permute-start.122 = (f32[256,512]{1,0:T(8,128)S(1)}, f32[256,512]{1,0:T(8,128)S(1)}, u32[]{:S(2)}, u32[]{:S(2)}) collective-permute-start(f32[256,512]{1,0:T(8,128)S(1)} %get-tuple-element.696), channel_id=1, source_target_pairs={{0,16},{1,5},{2,18},{3,7},{4,20},{5,9},{6,22},{7,11},{8,24},{9,13}... | collective-permute-start | bytes 1572872 | tf_op jit(solution)/shard_map/ppermute | solution.py:68
  447.9 18.0 %collective-permute-start.123 = (f32[256,512]{1,0:T(8,128)S(1)}, f32[256,512]{1,0:T(8,128)S(1)}, u32[]{:S(2)}, u32[]{:S(2)}) collective-permute-start(f32[256,512]{1,0:T(8,128)S(1)} %get-tuple-element.697), channel_id=1, source_target_pairs={{0,48},{1,13},{2,50},{3,15},{4,52},{5,1},{6,54},{7,3},{8,56},{9,5}... | collective-permute-start | bytes 1572872 | tf_op jit(solution)/shard_map/ppermute | solution.py:68
  (103 other events, 686.9 us)
